TPU v7x, 256 devices: a whole 4x4x8 slice. The times are simulated.
256 devices in a mesh: hst: 32 (over z, y), head: 8 (over x, core).
Axes of the slice: x: 4, y: 4, z: 8, core: 2. Of those that a mesh axis runs over, the one named last changes fastest.
Arguments:
- ctx_query: bfloat16 [32768, 8192], P(('hst', 'head')), may hold values from -180 to 180
- ctx_key: bfloat16 [32768, 1024], P(('hst', 'head')), may hold values from -6 to 6
- ctx_value: bfloat16 [32768, 1024], P(('hst', 'head')), may hold values from -6 to 6
- requests: bfloat16 [32, 256, 8192], P('hst', None, 'head'), may hold values from -180 to 180
- lengths: int32 [32], P('hst'), may hold values from 1 to 1024, as said below
- owner: int32 [32], replicated, may hold values from 0 to 31, each once
Outputs:
- context_out: bfloat16 [32768, 8192], P(('hst', 'head'))
- query_out: bfloat16 [256, 8192], P(None, 'head')
Inputs may be any that keep to these rules, and one draw needn't show every extreme that they name: `lengths`: every block holds 1024 live tokens except the last block.
All inputs are finite; a program needn't handle non-finite values.
Results may differ from a plain program's by a relative error of at most 0.0031.
Values may be sent and summed in bfloat16 or wider, within the bound.
No kernel may reach another device: no remote copies, remote signals or barrier semaphores. Data moves between devices by JAX's collectives and lax.ppermute only.
A program may use at most 128 MiB of HBM per device.

v0:
```python
import jax
import jax.numpy as jnp
from jax import lax
from jax.sharding import PartitionSpec as P

DH = 128


def spread(shard, axis, root):
    mine = lax.axis_index(axis) == root
    return lax.psum(jnp.where(mine, shard, jnp.zeros_like(shard)), axis)


def merged(part, axis, combine):
    gathered = jax.tree.map(lambda a: lax.all_gather(a, axis), part)

    def take(source):
        return jax.tree.map(lambda a: lax.dynamic_index_in_dim(a, source, 0, False), gathered)

    return lax.fori_loop(
        1, lax.axis_size(axis), lambda source, state: combine(state, take(source)), take(0)
    )


def head_attend(query_head, key_head, value_head, keep):
    scores = jnp.dot(query_head, key_head.T, preferred_element_type=jnp.float32) * DH ** (-0.5)
    scores = jnp.where(keep, scores, -1e30)
    top = jnp.max(scores, axis=1)
    weights = jnp.where(keep, jnp.exp(scores - top[:, None]), 0.0)
    total = jnp.sum(weights, axis=1)
    summed = jnp.dot(weights.astype(jnp.bfloat16), value_head, preferred_element_type=jnp.float32)
    return (top, total, summed)


def every_head(queries, keys, values, keep):
    heads = queries.shape[1] // DH

    def one_head(index):
        query_head = lax.dynamic_slice_in_dim(queries, index * DH, DH, 1)
        return head_attend(query_head, keys, values, keep)

    return lax.map(one_head, jnp.arange(heads, dtype=jnp.int32))


def combine_parts(first, second):
    best = jnp.maximum(first[0], second[0])
    weight_a = jnp.exp(first[0] - best)
    weight_b = jnp.exp(second[0] - best)
    return (
        best,
        first[1] * weight_a + second[1] * weight_b,
        first[2] * weight_a[..., None] + second[2] * weight_b[..., None],
    )


def per_device(ctx_query, ctx_key, ctx_value, requests, lengths, owner):
    block = ctx_query.shape[0] * lax.axis_size("head")
    front = block // 2
    queries, keys, values = (
        lax.all_to_all(ctx_query, "head", split_axis=1, concat_axis=0, tiled=True),
        lax.all_to_all(ctx_key, "head", split_axis=1, concat_axis=0, tiled=True),
        lax.all_to_all(ctx_value, "head", split_axis=1, concat_axis=0, tiled=True),
    )
    anchor_key, anchor_value = (spread(keys[:front], "hst", 0), spread(values[:front], "hst", 0))
    host = lax.axis_index("hst")
    length = lengths[0]
    positions = jnp.arange(block, dtype=jnp.int32)
    causal = (positions[None, :] <= positions[:, None]) & (positions[None, :] < length)
    leading = jnp.broadcast_to(host > 0, (block, front))
    keep = jnp.concatenate([leading, causal], axis=1)
    joined_key = jnp.concatenate([anchor_key, keys], axis=0)
    joined_value = jnp.concatenate([anchor_value, values], axis=0)
    top, total, summed = every_head(queries, joined_key, joined_value, keep)
    live = positions < length
    safe = jnp.where(live[None, :], total, 1.0)
    context = jnp.where(live[None, :, None], summed / safe[:, :, None], 0.0)
    context = context.transpose(1, 0, 2).reshape(block, -1).astype(jnp.bfloat16)
    context_out = lax.all_to_all(context, "head", split_axis=0, concat_axis=1, tiled=True)
    asked = spread(requests[0], "hst", owner[0])
    query_rows = asked.shape[0]
    key_keep = jnp.broadcast_to(live[None, :], (query_rows, block))
    top, total, summed = every_head(asked, keys, values, key_keep)
    top, total, summed = merged((top, total, summed), "hst", combine_parts)
    finished = (summed / total[..., None]).astype(jnp.bfloat16)
    query_out = finished.transpose(1, 0, 2).reshape(query_rows, -1)
    return (context_out, query_out)


def solution(mesh):
    placed = (
        P(("hst", "head"), None),
        P(("hst", "head"), None),
        P(("hst", "head"), None),
        P("hst", None, "head"),
        P("hst"),
        P(),
    )
    return jax.shard_map(
        per_device,
        mesh=mesh,
        in_specs=placed,
        out_specs=(P(("hst", "head"), None), P(None, "head")),
        check_vma=False,
    )
```

profile of v0, /device:TPU:1, one launch (start us, length us, event | category | flops | bytes accessed | tf_op | source)
XLA Modules:
  0.0 525.4 jit_solution(7509729661918472532)
XLA Ops:
  8.9 6.6 %all-to-all-start.1 = ((bf16[128,8,128]{2,0,1:T(8,128)(2,1)}), bf16[128,8,128]{2,0,1:T(8,128)(2,1)S(1)}, u32[]{:S(2)}, u32[]{:S(2)}) async-start(bf16[128,8,128]{2,0,1:T(8,128)(2,1)} %copy_bitcast_fusion.3), calls=%async_computation.1 | async-start | bytes 524288 | tf_op jit(solution)/shard_map/all_to_all | solution.py:61
  18.6 3.3 all-to-all-done.1
  22.0 4.4 all-to-all-start.2
  27.0 5.9 %all-to-all-done.2 = bf16[128,8,128]{2,0,1:T(8,128)(2,1)S(1)} async-done(((bf16[128,8,128]{2,0,1:T(8,128)(2,1)}), bf16[128,8,128]{2,0,1:T(8,128)(2,1)S(1)}, u32[]{:S(2)}, u32[]{:S(2)}) %all-to-all-start.2) | async-done | bytes 262176 | tf_op jit(solution)/shard_map/all_to_all | solution.py:62
  34.2 144.5 %all-reduce.4.cloned.1.call-done = (bf16[512,128]{1,0:T(8,128)(2,1)}, bf16[512,128]{1,0:T(8,128)(2,1)}, bf16[256,1024]{1,0:T(8,128)(2,1)}) async-done(((bf16[512,128]{1,0:T(8,128)(2,1)}, bf16[512,128]{1,0:T(8,128)(2,1)}, bf16[256,1024]{1,0:T(8,128)(2,1)}), (bf16[512,128]{1,0:T(8,128)(2,1)}, bf16[512,128]{1,0:T(8,128)(2,1)}, bf16[256,1024]{1,0:T(8,128)(2,1)})) %all-reduce.4.cloned.1.call-update) | async-done | bytes 786448 | tf_op jit(solution)/shard_map/psum | solution.py:11
  178.8 31.5 %while.51 = (s32[]{:T(128)}, f32[8,256]{1,0:T(8,128)S(1)}, f32[8,256]{1,0:T(8,128)S(1)}, f32[8,256,128]{2,1,0:T(8,128)}, s32[8]{0:T(128)S(1)}, /*index=5*/bf16[2...) while((s32[]{:T(128)}, f32[8,256]{1,0:T(8,128)S(1)}, ...), condition=%wide.region_10.11_spmd.clone.clone, body=%wide.region_7.10_spmd.clone.sunk.clone | while | flops 136576512 | bytes 3878571 | solution.py:42
  211.9 9.7 %all-to-all-start = ((bf16[128,8,1024]{2,0,1:T(8,128)(2,1)}), bf16[128,8,1024]{2,0,1:T(8,128)(2,1)}, u32[]{:S(2)}, u32[]{:S(2)}) async-start(bf16[128,8,1024]{2,0,1:T(8,128)(2,1)} %bitcast.73), calls=%async_computation | async-start | bytes 4194304 | tf_op jit(solution)/shard_map/all_to_all | solution.py:60
  222.8 25.3 %all-to-all-done = bf16[128,8,1024]{2,0,1:T(8,128)(2,1)} async-done(((bf16[128,8,1024]{2,0,1:T(8,128)(2,1)}), bf16[128,8,1024]{2,0,1:T(8,128)(2,1)}, u32[]{:S(2)}, u32[]{:S(2)}) %all-to-all-start) | async-done | bytes 2097184 | tf_op jit(solution)/shard_map/all_to_all | solution.py:60
  248.1 71.8 %while.49 = (s32[]{:T(128)}, f32[8,1024]{1,0:T(8,128)S(1)}, f32[8,1024,128]{2,1,0:T(8,128)}, s32[8]{0:T(128)S(1)}, bf16[1024,1024]{1,0:T(8,128)(2,1)}, /*index=5...) while((s32[]{:T(128)}, f32[8,1024]{1,0:T(8,128)S(1)}, ...), condition=%wide.region_5.6_spmd.clone, body=%wide.region_2.5_spmd.sunk.clone | while | flops 825751552 | bytes 25191072 | solution.py:42
  251.7 2.8 fusion.78
  260.7 2.8 fusion.78
  269.6 2.8 fusion.78
  278.6 2.8 fusion.78
  287.6 2.8 fusion.78
  296.6 2.8 fusion.78
  305.5 2.8 fusion.78
  314.5 2.8 fusion.78
  319.9 3.8 fusion.34
  327.4 4.4 all-to-all-start.3
  331.8 40.8 %all-gather = f32[256,256]{1,0:T(8,128)S(1)} all-gather(f32[8,256]{1,0:T(8,128)S(1)} %get-tuple-element.273), channel_id=2, replica_groups=mesh['hst'=32,'head'=8] {'hst'}, dimensions={0}, use_global_device_ids=true | all-gather | bytes 270336 | tf_op jit(solution)/shard_map/all_gather | solution.py:15
  372.5 40.5 %all-gather.1 = f32[256,256]{1,0:T(8,128)S(1)} all-gather(f32[8,256]{1,0:T(8,128)S(1)} %get-tuple-element.274), channel_id=3, replica_groups=mesh['hst'=32,'head'=8] {'hst'}, dimensions={0}, use_global_device_ids=true | all-gather | bytes 270336 | tf_op jit(solution)/shard_map/all_gather | solution.py:15
  415.4 4.1 copy.30
  419.5 29.0 %all-gather.5.cloned.1.call-done = f32[256,256,128]{2,1,0:T(8,128)} async-done(((f32[8,256,128]{2,1,0:T(8,128)}), f32[256,256,128]{2,1,0:T(8,128)}) %all-gather.5.cloned.1.call-update) | async-done | bytes 33554448 | tf_op jit(solution)/shard_map/all_gather | solution.py:15
  449.8 67.6 %while.50 = (s32[]{:T(128)}, f32[8,256]{1,0:T(8,128)S(1)}, f32[8,256]{1,0:T(8,128)S(1)}, f32[8,256,128]{2,1,0:T(8,128)S(1)}, f32[32,8,256]{2,1,0:T(8,128)S(1)}, ...) while((s32[]{:T(128)}, f32[8,256]{1,0:T(8,128)S(1)}, f32[8,256]{1,0:T(8,128)S(1)}, ...), condition=%wide.region_12.13_spmd.clone, body=%wide.region_11.12_spmd.sunk.clone | while | flops 798725 | bytes 3227775 | solution.py:20
  (183 shorter events, 153.4 us)
Async XLA Ops:
  7.2 1.0 copy-start
  8.9 13.1 %all-to-all-start.1 = ((bf16[128,8,128]{2,0,1:T(8,128)(2,1)}), bf16[128,8,128]{2,0,1:T(8,128)(2,1)S(1)}, u32[]{:S(2)}, u32[]{:S(2)}) async-start(bf16[128,8,128]{2,0,1:T(8,128)(2,1)} %copy_bitcast_fusion.3), calls=%async_computation.1 | async-start | bytes 524288 | tf_op jit(solution)/shard_map/all_to_all | solution.py:61
  22.0 10.9 %all-to-all-start.2 = ((bf16[128,8,128]{2,0,1:T(8,128)(2,1)}), bf16[128,8,128]{2,0,1:T(8,128)(2,1)S(1)}, u32[]{:S(2)}, u32[]{:S(2)}) async-start(bf16[128,8,128]{2,0,1:T(8,128)(2,1)} %copy_bitcast_fusion.2), calls=%async_computation.2 | async-start | bytes 524288 | tf_op jit(solution)/shard_map/all_to_all | solution.py:62
  26.3 152.4 %all-reduce.4.cloned.1.call-start = ((), (), s32[]{:S(2)}) async-start(), calls=%async_computation.5 | async-start | bytes 1572864 | tf_op jit(solution)/shard_map/psum | solution.py:11
  33.5 415.0 %all-gather.5.cloned.1.call-start = ((), (), s32[]{:S(2)}) async-start(), calls=%async_computation.4 | async-start | bytes 34603008 | tf_op jit(solution)/shard_map/all_gather | solution.py:15
  178.8 31.6 %copy-start.2 = (bf16[128,8192]{1,0:T(8,128)(2,1)S(1)}, bf16[128,8192]{1,0:T(8,128)(2,1)}, u32[]{:S(2)}) copy-start(bf16[128,8192]{1,0:T(8,128)(2,1)} %param.12) | copy-start | bytes 6291460
  211.9 36.2 %all-to-all-start = ((bf16[128,8,1024]{2,0,1:T(8,128)(2,1)}), bf16[128,8,1024]{2,0,1:T(8,128)(2,1)}, u32[]{:S(2)}, u32[]{:S(2)}) async-start(bf16[128,8,1024]{2,0,1:T(8,128)(2,1)} %bitcast.73), calls=%async_computation | async-start | bytes 4194304 | tf_op jit(solution)/shard_map/all_to_all | solution.py:60
  221.6 1.1 copy-start.3
  221.6 1.1 copy-start.4
  327.4 85.7 %all-to-all-start.3 = ((bf16[8,128,1024]{2,1,0:T(8,128)(2,1)}), bf16[8,128,1024]{2,1,0:T(8,128)(2,1)S(1)}, u32[]{:S(2)}, u32[]{:S(2)}) async-start(bf16[8,128,1024]{2,1,0:T(8,128)(2,1)} %convert_element_type.21), calls=%async_computation.3 | async-start | bytes 4194304 | tf_op jit(solution)/shard_map/all_to_all | solution.py:78
  517.4 1.2 copy-start.1
Sparse Core Ops, SparseCore 0:
  33.6 145.0 all-reduce.3
  210.5 238.0 all-gather.4
where the time goes:
time: 528 us; the launch traced here: 525 us
  waiting for transfers between devices  208 us (39%)
  other arithmetic  96 us (18%)
  blocking collectives  81.3 us (15%)
  matrix products  59.7 us (11%)
  local copies, waits for them, and re-layouts  28 us (5%)
  starting transfers between devices  25.1 us (5%)
  between operations  15.5 us (3%)
  loops' own time  11.9 us (2%)
    psum x1, waiting for transfers between devices, spread(): return lax.psum(jnp.where(mine, shard, jnp.zeros_like(shard)), axis)  145 us
    all_gather x2, blocking collectives, merged(): gathered = jax.tree.map(lambda a: lax.all_gather(a, axis), part)  81.3 us
    add x31, other arithmetic, combine_parts(): first[2] * weight_a[..., None] + second[2] * weight_b[..., None]  66 us
    dot_general x16, matrix products, head_attend(): jnp.dot(weights.astype(jnp.bfloat16), value_head, preferred_element_type=...  30.8 us
    all_gather x1, waiting for transfers between devices, merged(): gathered = jax.tree.map(lambda a: lax.all_gather(a, axis), part)  29 us
    dot_general x16, matrix products, head_attend(): jnp.dot(query_head, key_head.T, preferred_element_type=jnp.float32)  28.9 us
    all_to_all x1, waiting for transfers between devices, per_device(): lax.all_to_all(ctx_query, 'head', split_axis=1, concat_axis=0, tiled=True)  25.3 us
    reduce_sum x16, other arithmetic, head_attend(): total = jnp.sum(weights, axis=1)  21.8 us
  transfers between devices with their start and end apart: 6, of which 5 were waited for; matrix products, arithmetic and copies ran while one was open for 16% of the time, Pallas kernels for 0%

commit v1 on v0

v1 whole, which is shorter than its diff:
```python
import functools

import jax
import jax.numpy as jnp
from jax import lax
from jax.experimental import pallas as pl
from jax.experimental.pallas import tpu as pltpu
from jax.sharding import PartitionSpec as P

DH = 128
CORES = 2
NEG = -1e30
EXP2_SCALE = DH ** (-0.5) * 1.4426950408889634


def shift_chip(x, step, chips):
    size = chips * CORES
    return lax.ppermute(x, "head", [(i, (i + step * CORES) % size) for i in range(size)])


def swap_core(x, size):
    return lax.ppermute(x, "head", [(i, i ^ 1) for i in range(size)])


def spread_over_group(shard, chips):
    own = [shard] + [shift_chip(shard, step, chips) for step in range(1, chips)]
    return own + [swap_core(part, chips * CORES) for part in own]


def spread_anchor(kv, hst, head, n_hst, n_head):
    rows = kv.shape[0] // 2
    sources = n_head // 2
    lower, upper = kv[:rows], kv[rows:]
    moved = lax.ppermute(upper, ("hst", "head"), [(h, h + sources) for h in range(sources)])
    part = jnp.where(head < sources, lower, moved)
    ny, nz = 4, n_hst // 4
    z, y = hst // ny, hst % ny

    def send(x, pairs, axis_of):
        return lax.ppermute(x, "hst", [(axis_of(a), axis_of(b)) for a, b in pairs])

    along_z = lambda a: a * ny
    first, second = send(part, [(0, 3)], along_z), send(part, [(0, 5)], along_z)
    part = jnp.where(z == 3, first, jnp.where(z == 5, second, part))
    first = send(part, [(0, 1), (3, 4), (5, 6)], along_z)
    second = send(part, [(0, 7), (3, 2)], along_z)
    part = jnp.where((z == 1) | (z == 4) | (z == 6), first, jnp.where((z == 7) | (z == 2), second, part))
    for_y = [lax.ppermute(part, "hst", [(k * ny, k * ny + to) for k in range(nz)]) for to in (1, 3, 2)]
    return jnp.where(
        y == 1, for_y[0], jnp.where(y == 3, for_y[1], jnp.where(y == 2, for_y[2], part))
    )


def query_kernel(scal, asked, *refs):
    shards = 8
    keys, values, out = refs[:shards], refs[shards : 2 * shards], refs[2 * shards]
    length = scal[1]
    key = jnp.concatenate([r[...] for r in keys], axis=0)
    value = jnp.concatenate([r[...] for r in values], axis=0)
    rows = asked.shape[0]
    heads = asked.shape[1] // DH
    width = keys[0].shape[0]
    lane = lax.broadcasted_iota(jnp.int32, (1, width), 1)
    place = jnp.concatenate([lane + scal[2 + j] * width for j in range(shards)], axis=1)
    keep = place < length
    column = lax.broadcasted_iota(jnp.int32, (rows, DH), 1)
    stats = jnp.zeros((rows, DH), jnp.float32)
    for a in range(heads):
        query = asked[:, a * DH : (a + 1) * DH]
        score = lax.dot_general(query, key, (((1,), (1,)), ((), ())), preferred_element_type=jnp.float32)
        score = jnp.where(keep, score, NEG)
        top = jnp.max(score, axis=1, keepdims=True)
        weight = jnp.exp2((score - top) * EXP2_SCALE)
        total = jnp.sum(weight, axis=1, keepdims=True)
        summed = jnp.dot(weight.astype(jnp.bfloat16), value, preferred_element_type=jnp.float32)
        out[:, a * DH : (a + 1) * DH] = summed
        stats = jnp.where(column == a, top * EXP2_SCALE, stats)
        stats = jnp.where(column == heads + a, total, stats)
    out[:, heads * DH :] = stats


def query_part(scal, asked, shards):
    rows, cols = asked.shape
    width = shards[0].shape[0]
    kv_heads = shards[0].shape[1] // (2 * DH)
    key_spec = pl.BlockSpec((width, DH), lambda i, s: (0, s[0]))
    value_spec = pl.BlockSpec((width, DH), lambda i, s: (0, kv_heads + s[0]))
    return pl.pallas_call(
        query_kernel,
        out_shape=jax.ShapeDtypeStruct((rows, cols + DH), jnp.float32),
        grid_spec=pltpu.PrefetchScalarGridSpec(
            num_scalar_prefetch=1,
            grid=(1,),
            in_specs=[pl.BlockSpec((rows, cols), lambda i, s: (0, 0))]
            + [key_spec] * len(shards)
            + [value_spec] * len(shards),
            out_specs=pl.BlockSpec((rows, cols + DH), lambda i, s: (0, 0)),
        ),
        compiler_params=pltpu.CompilerParams(vmem_limit_bytes=40 * 2**20),
        cost_estimate=pl.CostEstimate(flops=2**31, bytes_accessed=2**22, transcendentals=2**21),
        name="query_part",
    )(scal, asked, *shards, *shards)


def merge_kernel(parts, out):
    heads = out.shape[1] // DH
    n = parts.shape[0]
    for a in range(heads):
        top = parts[:, :, heads * DH + a : heads * DH + a + 1]
        total = parts[:, :, heads * DH + heads + a : heads * DH + heads + a + 1]
        best = jnp.max(top, axis=0, keepdims=True)
        scale = jnp.exp2(top - best)
        total_all = jnp.sum(total * scale, axis=0)
        summed = jnp.sum(parts[:, :, a * DH : (a + 1) * DH] * scale, axis=0)
        out[:, a * DH : (a + 1) * DH] = (summed / total_all).astype(out.dtype)


def merge_parts(parts):
    n, rows, cols = parts.shape
    return pl.pallas_call(
        merge_kernel,
        out_shape=jax.ShapeDtypeStruct((rows, cols - DH), jnp.bfloat16),
        compiler_params=pltpu.CompilerParams(vmem_limit_bytes=40 * 2**20),
        cost_estimate=pl.CostEstimate(flops=2**20, bytes_accessed=2**21, transcendentals=2**10),
        name="merge_parts",
    )(parts)


def context_kernel(scal, query, *refs):
    shards = 8
    keys, values = refs[:shards], refs[shards : 2 * shards]
    front_keys, front_values = refs[2 * shards : 3 * shards], refs[3 * shards : 4 * shards]
    out = refs[4 * shards]
    own, length, hst = scal[0], scal[1], scal[10]
    rows = query.shape[0]
    heads = query.shape[1] // DH
    stack = 4
    many = stack * rows
    key = jnp.concatenate([r[...] for r in keys] + [r[...] for r in front_keys], axis=0)
    value = jnp.concatenate([r[...] for r in values] + [r[...] for r in front_values], axis=0)
    front = front_keys[0].shape[0] * shards
    row = lax.broadcasted_iota(jnp.int32, (many, rows), 0) % rows
    lane = lax.broadcasted_iota(jnp.int32, (many, rows), 1)
    diagonal = lane <= row
    bias = [jnp.zeros((1, rows), jnp.float32)]
    for j in range(1, shards):
        bias.append(jnp.full((1, rows), jnp.where(scal[2 + j] < own, 0.0, NEG), jnp.float32))
    bias.append(jnp.full((1, front), jnp.where(hst > 0, 0.0, NEG), jnp.float32))
    bias = jnp.concatenate(bias, axis=1)
    place = own * rows + lax.broadcasted_iota(jnp.int32, (many, 1), 0) % rows
    live = place < length
    for part in range(heads // stack):
        columns = [slice((part * stack + a) * DH, (part * stack + a + 1) * DH) for a in range(stack)]
        q = jnp.concatenate([query[:, c] for c in columns], axis=0)
        score = lax.dot_general(q, key, (((1,), (1,)), ((), ())), preferred_element_type=jnp.float32)
        score = jnp.concatenate(
            [jnp.where(diagonal, score[:, :rows], NEG), score[:, rows:] + bias[:, rows:]], axis=1
        )
        top = jnp.max(score, axis=1, keepdims=True)
        weight = jnp.exp2((score - top) * EXP2_SCALE)
        total = jnp.sum(weight, axis=1, keepdims=True)
        summed = jnp.dot(weight.astype(jnp.bfloat16), value, preferred_element_type=jnp.float32)
        result = jnp.where(live, summed / total, 0.0).astype(out.dtype)
        for a, c in enumerate(columns):
            out[:, c] = result[a * rows : (a + 1) * rows]


def context_part(scal, query, shards, fronts):
    rows, cols = query.shape
    kv_heads = shards[0].shape[1] // (2 * DH)
    group = cols // kv_heads

    def specs(parts, offset):
        return [
            pl.BlockSpec((p.shape[0], DH), lambda g, s: (0, g + offset)) for p in parts
        ]

    return pl.pallas_call(
        context_kernel,
        out_shape=jax.ShapeDtypeStruct((rows, cols), jnp.bfloat16),
        grid_spec=pltpu.PrefetchScalarGridSpec(
            num_scalar_prefetch=1,
            grid=(kv_heads,),
            in_specs=[pl.BlockSpec((rows, group), lambda g, s: (0, g))]
            + specs(shards, 0)
            + specs(shards, kv_heads)
            + specs(fronts, 0)
            + specs(fronts, kv_heads),
            out_specs=pl.BlockSpec((rows, group), lambda g, s: (0, g)),
        ),
        compiler_params=pltpu.CompilerParams(vmem_limit_bytes=48 * 2**20),
        cost_estimate=pl.CostEstimate(flops=2**34, bytes_accessed=2**23, transcendentals=2**24),
        name="context_part",
    )(scal, query, *shards, *shards, *fronts, *fronts)


def per_device(n_hst, n_head, ctx_query, ctx_key, ctx_value, requests, lengths, owner):
    hst, head = lax.axis_index("hst"), lax.axis_index("head")
    chips = n_head // CORES
    pieces = requests[0].reshape(n_hst, -1, requests.shape[2])
    scattered = lax.all_to_all(pieces, "hst", 0, 0)
    piece = lax.dynamic_index_in_dim(scattered, owner[0], 0, False)
    asked = lax.all_to_all(jnp.broadcast_to(piece[None], pieces.shape), "hst", 0, 0)
    asked = asked.reshape(requests.shape[1:])
    kv = jnp.concatenate([ctx_key, ctx_value], axis=1)
    shards = spread_over_group(kv, chips)
    fronts = spread_over_group(spread_anchor(kv, hst, head, n_hst, n_head), chips)
    x, core = head // CORES, head % CORES
    places = [((x - step) % chips) * CORES + c for c in (core, 1 - core) for step in range(chips)]
    scal = jnp.stack([head, lengths[0]] + places + [hst]).astype(jnp.int32)
    part = query_part(scal, asked, shards)
    parts = lax.all_to_all(part.reshape(n_hst, -1, part.shape[1]), "hst", 0, 0)
    context_out = context_part(scal, ctx_query, shards, fronts)
    done = merge_parts(parts)
    query_out = lax.all_to_all(jnp.broadcast_to(done[None], (n_hst,) + done.shape), "hst", 0, 0)
    return context_out, query_out.reshape(requests.shape[1:])


def solution(mesh):
    placed = (
        P(("hst", "head"), None),
        P(("hst", "head"), None),
        P(("hst", "head"), None),
        P("hst", None, "head"),
        P("hst"),
        P(),
    )
    return jax.shard_map(
        functools.partial(per_device, mesh.shape["hst"], mesh.shape["head"]),
        mesh=mesh,
        in_specs=placed,
        out_specs=(P(("hst", "head"), None), P(None, "head")),
        check_vma=False,
    )
```

time: 528 us -> 173 us (0.33)
  waiting for transfers between devices: 208 us -> 39.3 us
  other arithmetic: 96 us -> 2.79 us
  blocking collectives: 81.3 us -> 0 us
  matrix products: 59.7 us -> 0 us
  starting transfers between devices: 25.1 us -> 83 us
  Pallas kernels: 0 us -> 37.2 us
  local copies, waits for them, and re-layouts: 28 us -> 7.75 us
  between operations: 15.5 us -> 1.61 us
  loops' own time: 11.9 us -> 0 us
    psum x1 -> x0, waiting for transfers between devices: 145 us -> none  [spread(): return lax.psum(jnp.where(mine, shard, jnp.zeros_like(shard)), axis)]
    all_gather x2 -> x0, blocking collectives: 81.3 us -> none  [merged(): gathered = jax.tree.map(lambda a: lax.all_gather(a, axis), part)]
    add x62 -> x0, other arithmetic: 66.7 us -> none  [the longest x31 66 us: combine_parts(): first[2] * weight_a[..., None] + second[2] * weight_b[..., None]]
    dot_general x32 -> x0, matrix products: 59.7 us -> none  [the longest x16 30.8 us: head_attend(): jnp.dot(weights.astype(jnp.bfloat16), value_head, preferred_element_type=...]
    ppermute x0 -> x22, starting transfers between devices: none -> 47.3 us  [the longest x4 13.7 us: send(): return lax.ppermute(x, 'hst', [(axis_of(a), axis_of(b)) for a, b in pairs])]
    pallas_call x0 -> x3, Pallas kernels: none -> 37.2 us  [the longest x1 29.7 us: context_part(): pl.pallas_call(context_kernel, out_shape=jax.ShapeDtypeStruct((rows, cols...]
    ppermute x0 -> x22, waiting for transfers between devices: none -> 30 us  [the longest x4 21.8 us: send(): return lax.ppermute(x, 'hst', [(axis_of(a), axis_of(b)) for a, b in pairs])]
    all_gather x1 -> x0, waiting for transfers between devices: 29 us -> none  [merged(): gathered = jax.tree.map(lambda a: lax.all_gather(a, axis), part)]
  transfers between devices with their start and end apart: 6 -> 26, of which waited for: 5 -> 7; matrix products, arithmetic and copies ran while one was open for 16% -> 4% of each run, Pallas kernels for 0% -> 22%
where the time goes in v1:
time: 173 us; the launch traced here: 172 us
  starting transfers between devices  83 us (48%)
  waiting for transfers between devices  39.3 us (23%)
  Pallas kernels  37.2 us (22%)
  local copies, waits for them, and re-layouts  7.75 us (4%)
  other arithmetic  2.79 us (2%)
    pallas_call x1, Pallas kernels, context_part(): pl.pallas_call(context_kernel, out_shape=jax.ShapeDtypeStruct((rows, cols...  29.7 us
    ppermute x4, waiting for transfers between devices, send(): return lax.ppermute(x, 'hst', [(axis_of(a), axis_of(b)) for a, b in pairs])  21.8 us
    ppermute x4, starting transfers between devices, send(): return lax.ppermute(x, 'hst', [(axis_of(a), axis_of(b)) for a, b in pairs])  13.7 us
    all_to_all x1, starting transfers between devices, per_device(): lax.all_to_all(jnp.broadcast_to(done[None], (n_hst,) + done.shape), 'hst'...  13.4 us
    ppermute x8, starting transfers between devices, swap_core(): return lax.ppermute(x, 'head', [(i, i ^ 1) for i in range(size)])  12.4 us
    all_to_all x1, starting transfers between devices, per_device(): scattered = lax.all_to_all(pieces, 'hst', 0, 0)  12 us
    ppermute x6, starting transfers between devices, shift_chip(): lax.ppermute(x, 'head', [(i, (i + step * CORES) % size) for i in range(si...  9.77 us
    all_to_all x1, waiting for transfers between devices, per_device(): scattered = lax.all_to_all(pieces, 'hst', 0, 0)  9.32 us
  transfers between devices with their start and end apart: 26, of which 7 were waited for; matrix products, arithmetic and copies ran while one was open for 4% of the time, Pallas kernels for 22%

profile of v1, /device:TPU:1, one launch (start us, length us, event | category | flops | bytes accessed | tf_op | source)
XLA Modules:
  0.0 171.6 jit_solution(2267531933288247125)
XLA Ops:
  0.6 12.0 %all-to-all-start = ((bf16[32,8,1024]{2,1,0:T(8,128)(2,1)}), bf16[32,8,1024]{2,1,0:T(8,128)(2,1)S(1)}, u32[]{:S(2)}, u32[]{:S(2)}) async-start(bf16[32,8,1024]{2,1,0:T(8,128)(2,1)} %bitcast.18), calls=%async_computation | async-start | bytes 1048576 | tf_op jit(solution)/shard_map/all_to_all | solution.py:201
  15.9 2.5 %collective-permute-start.1 = (bf16[128,2048]{1,0:T(8,128)(2,1)S(1)}, bf16[128,2048]{1,0:T(8,128)(2,1)S(1)}, u32[]{:S(2)}, u32[]{:S(2)}) collective-permute-start(bf16[128,2048]{1,0:T(8,128)(2,1)S(1)} %constant_dynamic-update-slice_fusion.refs_0_.refs_8_), channel_id=1, source_target_pairs={{0,4},{1,5},{2,6},{3,7},{4,0},{5,1},{6,2},{7,3},{8,12},{9,13},{10,... | collective-permute-start | bytes 1572872 | tf_op jit(solution)/shard_map/ppermute | solution.py:18
  19.6 9.3 %all-to-all-done = bf16[32,8,1024]{2,1,0:T(8,128)(2,1)S(1)} async-done(((bf16[32,8,1024]{2,1,0:T(8,128)(2,1)}), bf16[32,8,1024]{2,1,0:T(8,128)(2,1)S(1)}, u32[]{:S(2)}, u32[]{:S(2)}) %all-to-all-start) | async-done | bytes 524320 | tf_op jit(solution)/shard_map/all_to_all | solution.py:201
  29.8 5.3 %all-to-all-start.1 = ((bf16[32,8,1024]{2,1,0:T(8,128)(2,1)}), bf16[32,8,1024]{2,1,0:T(8,128)(2,1)}, u32[]{:S(2)}, u32[]{:S(2)}) async-start(bf16[32,8,1024]{2,1,0:T(8,128)(2,1)} %broadcast_in_dim.7), calls=%async_computation.1 | async-start | bytes 1048576 | tf_op jit(solution)/shard_map/all_to_all | solution.py:203
  35.2 5.4 %collective-permute-start.7 = (bf16[64,2048]{1,0:T(8,128)(2,1)S(1)}, bf16[64,2048]{1,0:T(8,128)(2,1)}, u32[]{:S(2)}, u32[]{:S(2)}) collective-permute-start(bf16[64,2048]{1,0:T(8,128)(2,1)S(1)} %slice.13), channel_id=1, source_target_pairs={{0,4},{1,5},{2,6},{3,7}} | collective-permute-start | bytes 786440 | tf_op jit(solution)/shard_map/ppermute | solution.py:34
  40.6 2.1 %collective-permute-start.3 = (bf16[128,2048]{1,0:T(8,128)(2,1)S(1)}, bf16[128,2048]{1,0:T(8,128)(2,1)S(1)}, u32[]{:S(2)}, u32[]{:S(2)}) collective-permute-start(bf16[128,2048]{1,0:T(8,128)(2,1)S(1)} %constant_dynamic-update-slice_fusion.refs_0_.refs_8_), channel_id=1, source_target_pairs={{0,1},{1,0},{2,3},{3,2},{4,5},{5,4},{6,7},{7,6},{8,9},{9,8},{10,11... | collective-permute-start | bytes 1572872 | tf_op jit(solution)/shard_map/ppermute | solution.py:22
  43.6 4.6 %collective-permute-start.8 = (bf16[64,2048]{1,0:T(8,128)(2,1)S(1)}, bf16[64,2048]{1,0:T(8,128)(2,1)}, u32[]{:S(2)}, u32[]{:S(2)}) collective-permute-start(bf16[64,2048]{1,0:T(8,128)(2,1)S(1)} %slice_select_fusion), channel_id=1, source_target_pairs={{0,96},{1,97},{2,98},{3,99},{4,100},{5,101},{6,102},{7,103}} | collective-permute-start | bytes 786440 | tf_op jit(solution)/shard_map/ppermute | solution.py:40
  48.2 2.6 %collective-permute-start.9 = (bf16[64,2048]{1,0:T(8,128)(2,1)S(1)}, bf16[64,2048]{1,0:T(8,128)(2,1)}, u32[]{:S(2)}, u32[]{:S(2)}) collective-permute-start(bf16[64,2048]{1,0:T(8,128)(2,1)S(1)} %slice_select_fusion), channel_id=1, source_target_pairs={{0,160},{1,161},{2,162},{3,163},{4,164},{5,165},{6,166},{7,167}} | collective-permute-start | bytes 786440 | tf_op jit(solution)/shard_map/ppermute | solution.py:40
  51.6 6.7 %query_part.1 = f32[256,1152]{1,0:T(8,128)} custom-call(s32[11]{0:T(128)S(1)} %stack.43.scal, bf16[256,1024]{1,0:T(8,128)(2,1)} %bitcast.13.asked, bf16[128,2048]{1,0:T(8,128)(2,1)S(1)} %constant_dynamic-update-slice_fusion.refs_0_.refs_8_, bf16[128,2048]{1,0:T(8,128)(2,1)S(1)} %collective-permute-done.refs_1_.refs_9_, ...), custom_call_target="tpu_custom_call" | custom-call | flops 2147483648 | bytes 4194304 | tf_op jit(solution)/shard_map/query_part/pallas_call | solution.py:88
  58.3 5.0 %all-to-all-start.2 = ((f32[32,8,1152]{2,1,0:T(8,128)}), f32[32,8,1152]{2,1,0:T(8,128)S(1)}, u32[]{:S(2)}, u32[]{:S(2)}) async-start(f32[32,8,1152]{2,1,0:T(8,128)} %bitcast.14), calls=%async_computation.2 | async-start | bytes 2359296 | tf_op jit(solution)/shard_map/all_to_all | solution.py:212
  64.3 3.9 %collective-permute-start.10 = (bf16[64,2048]{1,0:T(8,128)(2,1)S(1)}, bf16[64,2048]{1,0:T(8,128)(2,1)}, u32[]{:S(2)}, u32[]{:S(2)}) collective-permute-start(bf16[64,2048]{1,0:T(8,128)(2,1)S(1)} %select_select_fusion.2), channel_id=1, source_target_pairs={{0,32},{96,128},{160,192},{1,33},{97,129},{161,193},{2,34},{98,130... | collective-permute-start | bytes 786440 | tf_op jit(solution)/shard_map/ppermute | solution.py:40
  68.2 2.6 %collective-permute-start.11 = (bf16[64,2048]{1,0:T(8,128)(2,1)S(1)}, bf16[64,2048]{1,0:T(8,128)(2,1)}, u32[]{:S(2)}, u32[]{:S(2)}) collective-permute-start(bf16[64,2048]{1,0:T(8,128)(2,1)S(1)} %select_select_fusion.2), channel_id=1, source_target_pairs={{0,224},{96,64},{1,225},{97,65},{2,226},{98,66},{3,227},{99,67},{4... | collective-permute-start | bytes 786440 | tf_op jit(solution)/shard_map/ppermute | solution.py:40
  70.8 21.7 %collective-permute-done.10 = bf16[64,2048]{1,0:T(8,128)(2,1)} collective-permute-done((bf16[64,2048]{1,0:T(8,128)(2,1)S(1)}, bf16[64,2048]{1,0:T(8,128)(2,1)}, u32[]{:S(2)}, u32[]{:S(2)}) %collective-permute-start.10) | collective-permute-done | bytes 262176 | tf_op jit(solution)/shard_map/ppermute | solution.py:40
  93.4 2.0 %collective-permute-start.12 = (bf16[64,2048]{1,0:T(8,128)(2,1)}, bf16[64,2048]{1,0:T(8,128)(2,1)}, u32[]{:S(2)}, u32[]{:S(2)}) collective-permute-start(bf16[64,2048]{1,0:T(8,128)(2,1)} %select_select_fusion.1), channel_id=1, source_target_pairs={{0,8},{32,40},{64,72},{96,104},{128,136},{160,168},{192,200},{224,... | collective-permute-start | bytes 786440 | tf_op jit(solution)/shard_map/ppermute | solution.py:48
  95.4 2.0 %collective-permute-start.13 = (bf16[64,2048]{1,0:T(8,128)(2,1)}, bf16[64,2048]{1,0:T(8,128)(2,1)}, u32[]{:S(2)}, u32[]{:S(2)}) collective-permute-start(bf16[64,2048]{1,0:T(8,128)(2,1)} %select_select_fusion.1), channel_id=1, source_target_pairs={{0,24},{32,56},{64,88},{96,120},{128,152},{160,184},{192,216},{224... | collective-permute-start | bytes 786440 | tf_op jit(solution)/shard_map/ppermute | solution.py:48
  97.4 2.0 %collective-permute-start.14 = (bf16[64,2048]{1,0:T(8,128)(2,1)}, bf16[64,2048]{1,0:T(8,128)(2,1)}, u32[]{:S(2)}, u32[]{:S(2)}) collective-permute-start(bf16[64,2048]{1,0:T(8,128)(2,1)} %select_select_fusion.1), channel_id=1, source_target_pairs={{0,16},{32,48},{64,80},{96,112},{128,144},{160,176},{192,208},{224... | collective-permute-start | bytes 786440 | tf_op jit(solution)/shard_map/ppermute | solution.py:48
  100.3 4.8 %collective-permute-done.14 = bf16[64,2048]{1,0:T(8,128)(2,1)} collective-permute-done((bf16[64,2048]{1,0:T(8,128)(2,1)}, bf16[64,2048]{1,0:T(8,128)(2,1)}, u32[]{:S(2)}, u32[]{:S(2)}) %collective-permute-start.14) | collective-permute-done | bytes 262176 | tf_op jit(solution)/shard_map/ppermute | solution.py:48
  107.4 2.4 %collective-permute-start.16 = (bf16[64,2048]{1,0:T(8,128)(2,1)S(1)}, bf16[64,2048]{1,0:T(8,128)(2,1)}, u32[]{:S(2)}, u32[]{:S(2)}) collective-permute-start(bf16[64,2048]{1,0:T(8,128)(2,1)S(1)} %select_select_fusion.refs_16_.refs_24_), channel_id=1, source_target_pairs={{0,4},{1,5},{2,6},{3,7},{4,0},{5,1},{6,2},{7,3},{8,12},{9,13},{10,... | collective-permute-start | bytes 786440 | tf_op jit(solution)/shard_map/ppermute | solution.py:18
  111.0 2.8 %collective-permute-start.18 = (bf16[64,2048]{1,0:T(8,128)(2,1)S(1)}, bf16[64,2048]{1,0:T(8,128)(2,1)}, u32[]{:S(2)}, u32[]{:S(2)}) collective-permute-start(bf16[64,2048]{1,0:T(8,128)(2,1)S(1)} %select_select_fusion.refs_16_.refs_24_), channel_id=1, source_target_pairs={{0,1},{1,0},{2,3},{3,2},{4,5},{5,4},{6,7},{7,6},{8,9},{9,8},{10,11... | collective-permute-start | bytes 786440 | tf_op jit(solution)/shard_map/ppermute | solution.py:22
  113.8 3.9 %collective-permute-start.19 = (bf16[64,2048]{1,0:T(8,128)(2,1)}, bf16[64,2048]{1,0:T(8,128)(2,1)}, u32[]{:S(2)}, u32[]{:S(2)}) collective-permute-start(bf16[64,2048]{1,0:T(8,128)(2,1)} %collective-permute-done.15.refs_17_.refs_25_), channel_id=1, source_target_pairs={{0,1},{1,0},{2,3},{3,2},{4,5},{5,4},{6,7},{7,6},{8,9},{9,8},{10,11... | collective-permute-start | bytes 786440 | tf_op jit(solution)/shard_map/ppermute | solution.py:22
  117.8 2.1 %collective-permute-done.16.refs_18_.refs_26_ = bf16[64,2048]{1,0:T(8,128)(2,1)} collective-permute-done((bf16[64,2048]{1,0:T(8,128)(2,1)S(1)}, bf16[64,2048]{1,0:T(8,128)(2,1)}, u32[]{:S(2)}, u32[]{:S(2)}) %collective-permute-start.16) | collective-permute-done | bytes 262176 | tf_op jit(solution)/shard_map/ppermute | solution.py:18
  119.9 2.9 %collective-permute-start.20 = (bf16[64,2048]{1,0:T(8,128)(2,1)}, bf16[64,2048]{1,0:T(8,128)(2,1)}, u32[]{:S(2)}, u32[]{:S(2)}) collective-permute-start(bf16[64,2048]{1,0:T(8,128)(2,1)} %collective-permute-done.16.refs_18_.refs_26_), channel_id=1, source_target_pairs={{0,1},{1,0},{2,3},{3,2},{4,5},{5,4},{6,7},{7,6},{8,9},{9,8},{10,11... | collective-permute-start | bytes 786440 | tf_op jit(solution)/shard_map/ppermute | solution.py:22
  124.6 13.4 %all-to-all-start.3 = ((bf16[32,8,1024]{2,1,0:T(8,128)(2,1)}), bf16[32,8,1024]{2,1,0:T(8,128)(2,1)}, u32[]{:S(2)}, u32[]{:S(2)}) async-start(bf16[32,8,1024]{2,1,0:T(8,128)(2,1)} %broadcast_in_dim.16), calls=%async_computation.3 | async-start | bytes 1048576 | tf_op jit(solution)/shard_map/all_to_all | solution.py:215
  140.1 29.7 %context_part.1 = bf16[128,8192]{1,0:T(8,128)(2,1)} custom-call(s32[11]{0:T(128)S(1)} %stack.43.scal, bf16[128,8192]{1,0:T(8,128)(2,1)} %query.1, bf16[128,2048]{1,0:T(8,128)(2,1)S(1)} %constant_dynamic-update-slice_fusion.refs_0_.refs_8_, bf16[128,2048]{1,0:T(8,128)(2,1)S(1)} %collective-permute-done.refs_1_.refs_9_, ...), custom_call_target="tpu_custom_call" | custom-call | flops 17179869184 | bytes 8388608 | tf_op jit(solution)/shard_map/context_part/pallas_call | solution.py:178
  (55 shorter events, 18.2 us)
Async XLA Ops:
  0.6 28.3 %all-to-all-start = ((bf16[32,8,1024]{2,1,0:T(8,128)(2,1)}), bf16[32,8,1024]{2,1,0:T(8,128)(2,1)S(1)}, u32[]{:S(2)}, u32[]{:S(2)}) async-start(bf16[32,8,1024]{2,1,0:T(8,128)(2,1)} %bitcast.18), calls=%async_computation | async-start | bytes 1048576 | tf_op jit(solution)/shard_map/all_to_all | solution.py:201
  14.6 28.1 %collective-permute-start = (bf16[128,2048]{1,0:T(8,128)(2,1)S(1)}, bf16[128,2048]{1,0:T(8,128)(2,1)S(1)}, u32[]{:S(2)}, u32[]{:S(2)}) collective-permute-start(bf16[128,2048]{1,0:T(8,128)(2,1)S(1)} %constant_dynamic-update-slice_fusion.refs_0_.refs_8_), channel_id=1, source_target_pairs={{0,2},{1,3},{2,4},{3,5},{4,6},{5,7},{6,0},{7,1},{8,10},{9,11},{10,... | collective-permute-start | bytes 1572872 | tf_op jit(solution)/shard_map/ppermute | solution.py:18
  15.9 26.8 %collective-permute-start.1 = (bf16[128,2048]{1,0:T(8,128)(2,1)S(1)}, bf16[128,2048]{1,0:T(8,128)(2,1)S(1)}, u32[]{:S(2)}, u32[]{:S(2)}) collective-permute-start(bf16[128,2048]{1,0:T(8,128)(2,1)S(1)} %constant_dynamic-update-slice_fusion.refs_0_.refs_8_), channel_id=1, source_target_pairs={{0,4},{1,5},{2,6},{3,7},{4,0},{5,1},{6,2},{7,3},{8,12},{9,13},{10,... | collective-permute-start | bytes 1572872 | tf_op jit(solution)/shard_map/ppermute | solution.py:18
  18.4 24.9 %collective-permute-start.2 = (bf16[128,2048]{1,0:T(8,128)(2,1)S(1)}, bf16[128,2048]{1,0:T(8,128)(2,1)S(1)}, u32[]{:S(2)}, u32[]{:S(2)}) collective-permute-start(bf16[128,2048]{1,0:T(8,128)(2,1)S(1)} %constant_dynamic-update-slice_fusion.refs_0_.refs_8_), channel_id=1, source_target_pairs={{0,6},{1,7},{2,0},{3,1},{4,2},{5,3},{6,4},{7,5},{8,14},{9,15},{10,... | collective-permute-start | bytes 1572872 | tf_op jit(solution)/shard_map/ppermute | solution.py:18
  29.8 21.8 %all-to-all-start.1 = ((bf16[32,8,1024]{2,1,0:T(8,128)(2,1)}), bf16[32,8,1024]{2,1,0:T(8,128)(2,1)}, u32[]{:S(2)}, u32[]{:S(2)}) async-start(bf16[32,8,1024]{2,1,0:T(8,128)(2,1)} %broadcast_in_dim.7), calls=%async_computation.1 | async-start | bytes 1048576 | tf_op jit(solution)/shard_map/all_to_all | solution.py:203
  35.2 8.4 %collective-permute-start.7 = (bf16[64,2048]{1,0:T(8,128)(2,1)S(1)}, bf16[64,2048]{1,0:T(8,128)(2,1)}, u32[]{:S(2)}, u32[]{:S(2)}) collective-permute-start(bf16[64,2048]{1,0:T(8,128)(2,1)S(1)} %slice.13), channel_id=1, source_target_pairs={{0,4},{1,5},{2,6},{3,7}} | collective-permute-start | bytes 786440 | tf_op jit(solution)/shard_map/ppermute | solution.py:34
  40.6 7.6 %collective-permute-start.3 = (bf16[128,2048]{1,0:T(8,128)(2,1)S(1)}, bf16[128,2048]{1,0:T(8,128)(2,1)S(1)}, u32[]{:S(2)}, u32[]{:S(2)}) collective-permute-start(bf16[128,2048]{1,0:T(8,128)(2,1)S(1)} %constant_dynamic-update-slice_fusion.refs_0_.refs_8_), channel_id=1, source_target_pairs={{0,1},{1,0},{2,3},{3,2},{4,5},{5,4},{6,7},{7,6},{8,9},{9,8},{10,11... | collective-permute-start | bytes 1572872 | tf_op jit(solution)/shard_map/ppermute | solution.py:22
  42.7 8.8 %collective-permute-start.4 = (bf16[128,2048]{1,0:T(8,128)(2,1)S(1)}, bf16[128,2048]{1,0:T(8,128)(2,1)S(1)}, u32[]{:S(2)}, u32[]{:S(2)}) collective-permute-start(bf16[128,2048]{1,0:T(8,128)(2,1)S(1)} %collective-permute-done.refs_1_.refs_9_), channel_id=1, source_target_pairs={{0,1},{1,0},{2,3},{3,2},{4,5},{5,4},{6,7},{7,6},{8,9},{9,8},{10,11... | collective-permute-start | bytes 1572872 | tf_op jit(solution)/shard_map/ppermute | solution.py:22
  42.7 8.8 %collective-permute-start.5 = (bf16[128,2048]{1,0:T(8,128)(2,1)S(1)}, bf16[128,2048]{1,0:T(8,128)(2,1)}, u32[]{:S(2)}, u32[]{:S(2)}) collective-permute-start(bf16[128,2048]{1,0:T(8,128)(2,1)S(1)} %collective-permute-done.1.refs_2_.refs_10_), channel_id=1, source_target_pairs={{0,1},{1,0},{2,3},{3,2},{4,5},{5,4},{6,7},{7,6},{8,9},{9,8},{10,11... | collective-permute-start | bytes 1572872 | tf_op jit(solution)/shard_map/ppermute | solution.py:22
  43.2 8.3 %collective-permute-start.6 = (bf16[128,2048]{1,0:T(8,128)(2,1)S(1)}, bf16[128,2048]{1,0:T(8,128)(2,1)}, u32[]{:S(2)}, u32[]{:S(2)}) collective-permute-start(bf16[128,2048]{1,0:T(8,128)(2,1)S(1)} %collective-permute-done.2.refs_3_.refs_11_), channel_id=1, source_target_pairs={{0,1},{1,0},{2,3},{3,2},{4,5},{5,4},{6,7},{7,6},{8,9},{9,8},{10,11... | collective-permute-start | bytes 1572872 | tf_op jit(solution)/shard_map/ppermute | solution.py:22
  43.6 19.7 %collective-permute-start.8 = (bf16[64,2048]{1,0:T(8,128)(2,1)S(1)}, bf16[64,2048]{1,0:T(8,128)(2,1)}, u32[]{:S(2)}, u32[]{:S(2)}) collective-permute-start(bf16[64,2048]{1,0:T(8,128)(2,1)S(1)} %slice_select_fusion), channel_id=1, source_target_pairs={{0,96},{1,97},{2,98},{3,99},{4,100},{5,101},{6,102},{7,103}} | collective-permute-start | bytes 786440 | tf_op jit(solution)/shard_map/ppermute | solution.py:40
  48.2 15.1 %collective-permute-start.9 = (bf16[64,2048]{1,0:T(8,128)(2,1)S(1)}, bf16[64,2048]{1,0:T(8,128)(2,1)}, u32[]{:S(2)}, u32[]{:S(2)}) collective-permute-start(bf16[64,2048]{1,0:T(8,128)(2,1)S(1)} %slice_select_fusion), channel_id=1, source_target_pairs={{0,160},{1,161},{2,162},{3,163},{4,164},{5,165},{6,166},{7,167}} | collective-permute-start | bytes 786440 | tf_op jit(solution)/shard_map/ppermute | solution.py:40
  58.3 64.5 %all-to-all-start.2 = ((f32[32,8,1152]{2,1,0:T(8,128)}), f32[32,8,1152]{2,1,0:T(8,128)S(1)}, u32[]{:S(2)}, u32[]{:S(2)}) async-start(f32[32,8,1152]{2,1,0:T(8,128)} %bitcast.14), calls=%async_computation.2 | async-start | bytes 2359296 | tf_op jit(solution)/shard_map/all_to_all | solution.py:212
  64.3 28.2 %collective-permute-start.10 = (bf16[64,2048]{1,0:T(8,128)(2,1)S(1)}, bf16[64,2048]{1,0:T(8,128)(2,1)}, u32[]{:S(2)}, u32[]{:S(2)}) collective-permute-start(bf16[64,2048]{1,0:T(8,128)(2,1)S(1)} %select_select_fusion.2), channel_id=1, source_target_pairs={{0,32},{96,128},{160,192},{1,33},{97,129},{161,193},{2,34},{98,130... | collective-permute-start | bytes 786440 | tf_op jit(solution)/shard_map/ppermute | solution.py:40
  68.2 24.5 %collective-permute-start.11 = (bf16[64,2048]{1,0:T(8,128)(2,1)S(1)}, bf16[64,2048]{1,0:T(8,128)(2,1)}, u32[]{:S(2)}, u32[]{:S(2)}) collective-permute-start(bf16[64,2048]{1,0:T(8,128)(2,1)S(1)} %select_select_fusion.2), channel_id=1, source_target_pairs={{0,224},{96,64},{1,225},{97,65},{2,226},{98,66},{3,227},{99,67},{4... | collective-permute-start | bytes 786440 | tf_op jit(solution)/shard_map/ppermute | solution.py:40
  97.4 7.8 %collective-permute-start.14 = (bf16[64,2048]{1,0:T(8,128)(2,1)}, bf16[64,2048]{1,0:T(8,128)(2,1)}, u32[]{:S(2)}, u32[]{:S(2)}) collective-permute-start(bf16[64,2048]{1,0:T(8,128)(2,1)} %select_select_fusion.1), channel_id=1, source_target_pairs={{0,16},{32,48},{64,80},{96,112},{128,144},{160,176},{192,208},{224... | collective-permute-start | bytes 786440 | tf_op jit(solution)/shard_map/ppermute | solution.py:48
  106.1 7.7 %collective-permute-start.15 = (bf16[64,2048]{1,0:T(8,128)(2,1)S(1)}, bf16[64,2048]{1,0:T(8,128)(2,1)}, u32[]{:S(2)}, u32[]{:S(2)}) collective-permute-start(bf16[64,2048]{1,0:T(8,128)(2,1)S(1)} %select_select_fusion.refs_16_.refs_24_), channel_id=1, source_target_pairs={{0,2},{1,3},{2,4},{3,5},{4,6},{5,7},{6,0},{7,1},{8,10},{9,11},{10,... | collective-permute-start | bytes 786440 | tf_op jit(solution)/shard_map/ppermute | solution.py:18
  107.4 12.5 %collective-permute-start.16 = (bf16[64,2048]{1,0:T(8,128)(2,1)S(1)}, bf16[64,2048]{1,0:T(8,128)(2,1)}, u32[]{:S(2)}, u32[]{:S(2)}) collective-permute-start(bf16[64,2048]{1,0:T(8,128)(2,1)S(1)} %select_select_fusion.refs_16_.refs_24_), channel_id=1, source_target_pairs={{0,4},{1,5},{2,6},{3,7},{4,0},{5,1},{6,2},{7,3},{8,12},{9,13},{10,... | collective-permute-start | bytes 786440 | tf_op jit(solution)/shard_map/ppermute | solution.py:18
  109.8 13.0 %collective-permute-start.17 = (bf16[64,2048]{1,0:T(8,128)(2,1)S(1)}, bf16[64,2048]{1,0:T(8,128)(2,1)}, u32[]{:S(2)}, u32[]{:S(2)}) collective-permute-start(bf16[64,2048]{1,0:T(8,128)(2,1)S(1)} %select_select_fusion.refs_16_.refs_24_), channel_id=1, source_target_pairs={{0,6},{1,7},{2,0},{3,1},{4,2},{5,3},{6,4},{7,5},{8,14},{9,15},{10,... | collective-permute-start | bytes 786440 | tf_op jit(solution)/shard_map/ppermute | solution.py:18
  111.0 27.0 %collective-permute-start.18 = (bf16[64,2048]{1,0:T(8,128)(2,1)S(1)}, bf16[64,2048]{1,0:T(8,128)(2,1)}, u32[]{:S(2)}, u32[]{:S(2)}) collective-permute-start(bf16[64,2048]{1,0:T(8,128)(2,1)S(1)} %select_select_fusion.refs_16_.refs_24_), channel_id=1, source_target_pairs={{0,1},{1,0},{2,3},{3,2},{4,5},{5,4},{6,7},{7,6},{8,9},{9,8},{10,11... | collective-permute-start | bytes 786440 | tf_op jit(solution)/shard_map/ppermute | solution.py:22
  113.8 24.1 %collective-permute-start.19 = (bf16[64,2048]{1,0:T(8,128)(2,1)}, bf16[64,2048]{1,0:T(8,128)(2,1)}, u32[]{:S(2)}, u32[]{:S(2)}) collective-permute-start(bf16[64,2048]{1,0:T(8,128)(2,1)} %collective-permute-done.15.refs_17_.refs_25_), channel_id=1, source_target_pairs={{0,1},{1,0},{2,3},{3,2},{4,5},{5,4},{6,7},{7,6},{8,9},{9,8},{10,11... | collective-permute-start | bytes 786440 | tf_op jit(solution)/shard_map/ppermute | solution.py:22
  119.9 18.1 %collective-permute-start.20 = (bf16[64,2048]{1,0:T(8,128)(2,1)}, bf16[64,2048]{1,0:T(8,128)(2,1)}, u32[]{:S(2)}, u32[]{:S(2)}) collective-permute-start(bf16[64,2048]{1,0:T(8,128)(2,1)} %collective-permute-done.16.refs_18_.refs_26_), channel_id=1, source_target_pairs={{0,1},{1,0},{2,3},{3,2},{4,5},{5,4},{6,7},{7,6},{8,9},{9,8},{10,11... | collective-permute-start | bytes 786440 | tf_op jit(solution)/shard_map/ppermute | solution.py:22
  122.8 15.2 %collective-permute-start.21 = (bf16[64,2048]{1,0:T(8,128)(2,1)}, bf16[64,2048]{1,0:T(8,128)(2,1)}, u32[]{:S(2)}, u32[]{:S(2)}) collective-permute-start(bf16[64,2048]{1,0:T(8,128)(2,1)} %collective-permute-done.17.refs_19_.refs_27_), channel_id=1, source_target_pairs={{0,1},{1,0},{2,3},{3,2},{4,5},{5,4},{6,7},{7,6},{8,9},{9,8},{10,11... | collective-permute-start | bytes 786440 | tf_op jit(solution)/shard_map/ppermute | solution.py:22
  124.6 45.2 %all-to-all-start.3 = ((bf16[32,8,1024]{2,1,0:T(8,128)(2,1)}), bf16[32,8,1024]{2,1,0:T(8,128)(2,1)}, u32[]{:S(2)}, u32[]{:S(2)}) async-start(bf16[32,8,1024]{2,1,0:T(8,128)(2,1)} %broadcast_in_dim.16), calls=%async_computation.3 | async-start | bytes 1048576 | tf_op jit(solution)/shard_map/all_to_all | solution.py:215
  (8 other events, 63.4 us)

commit v2 on v1

v2 whole, which is shorter than its diff:
```python
import functools

import jax
import jax.numpy as jnp
from jax import lax
from jax.experimental import pallas as pl
from jax.experimental.pallas import tpu as pltpu
from jax.sharding import PartitionSpec as P

DH = 128
CORES = 2
NEG = -1e30
EXP2_SCALE = DH ** (-0.5) * 1.4426950408889634


def spread_over_group(shard, chips):
    size = chips * CORES
    ring = [
        lax.ppermute(shard, "head", [(i, (i + step * CORES) % size) for i in range(size)])
        for step in range(1, chips)
    ]
    near = jnp.concatenate([shard] + ring, axis=0)
    return near, lax.ppermute(near, "head", [(i, i ^ 1) for i in range(size)])


def spread_anchor(kv, hst, head, n_hst, n_head, ny):
    rows = kv.shape[0] // 2
    sources = n_head // 2
    moved = lax.ppermute(kv[rows:], ("hst", "head"), [(h, h + sources) for h in range(sources)])
    part = jnp.where(head < sources, kv[:rows], moved)
    z, y = hst // ny, hst % ny

    def send(x, pairs):
        return lax.ppermute(x, "hst", [(a * ny, b * ny) for a, b in pairs])

    first, second = send(part, [(0, 3)]), send(part, [(0, 5)])
    part = jnp.where(z == 3, first, jnp.where(z == 5, second, part))
    first, second = send(part, [(0, 1), (3, 4), (5, 6)]), send(part, [(0, 7), (3, 2)])
    part = jnp.where((z == 1) | (z == 4) | (z == 6), first, jnp.where((z == 7) | (z == 2), second, part))
    groups = range(n_hst // ny)
    first, second, third = (
        lax.ppermute(part, "hst", [(k * ny, k * ny + to) for k in groups]) for to in (1, 3, 2)
    )
    return jnp.where(y == 1, first, jnp.where(y == 3, second, jnp.where(y == 2, third, part)))


def pieces_of(x):
    parts = []
    for _ in range(3):
        parts.append(x.astype(jnp.bfloat16).astype(jnp.float32))
        x = x - parts[-1]
    return parts


def query_kernel(shards, scal, asked, near_key, far_key, near_value, far_value, after, out):
    length = scal[1]
    rows, heads = asked.shape[0], asked.shape[1] // DH
    key = jnp.concatenate([near_key[...], far_key[...]], axis=0)
    value = jnp.concatenate([near_value[...], far_value[...]], axis=0)
    width = key.shape[0] // shards
    lane = lax.broadcasted_iota(jnp.int32, (1, width), 1)
    keep = jnp.concatenate([lane + scal[3 + j] * width for j in range(shards)], axis=1) < length
    column = lax.broadcasted_iota(jnp.int32, (rows, DH), 1)
    stats = jnp.zeros((rows, DH), jnp.float32)
    for a in range(heads):
        query = asked[:, a * DH : (a + 1) * DH]
        score = lax.dot_general(query, key, (((1,), (1,)), ((), ())), preferred_element_type=jnp.float32)
        score = jnp.where(keep, score, NEG)
        top = jnp.max(score, axis=1, keepdims=True)
        weight = jnp.exp2((score - top) * EXP2_SCALE)
        total = jnp.sum(weight, axis=1, keepdims=True)
        summed = jnp.dot(weight.astype(jnp.bfloat16), value, preferred_element_type=jnp.float32)
        reach = jnp.max(jnp.abs(summed), axis=1, keepdims=True)
        power = jnp.ceil(jnp.log2(jnp.maximum(reach, 1e-36)))
        out[:, a * DH : (a + 1) * DH] = summed * jnp.exp2(-power)
        values = pieces_of(top * EXP2_SCALE) + pieces_of(total) + [power]
        for at, stat in enumerate(values):
            stats = jnp.where(column == at * heads + a, stat, stats)
    out[:, heads * DH :] = stats


def query_part(scal, asked, near, far, shards, after):
    rows, cols = asked.shape
    width = near.shape[0]
    kv_heads = near.shape[1] // (2 * DH)
    key = pl.BlockSpec((width, DH), lambda i, s: (0, s[0]))
    value = pl.BlockSpec((width, DH), lambda i, s: (0, kv_heads + s[0]))
    return pl.pallas_call(
        functools.partial(query_kernel, shards),
        out_shape=jax.ShapeDtypeStruct((rows, cols + DH), jnp.float32),
        grid_spec=pltpu.PrefetchScalarGridSpec(
            num_scalar_prefetch=1,
            grid=(1,),
            in_specs=[
                pl.BlockSpec((rows, cols), lambda i, s: (0, 0)),
                key,
                key,
                value,
                value,
                pl.BlockSpec(memory_space=pl.ANY),
            ],
            out_specs=pl.BlockSpec((rows, cols + DH), lambda i, s: (0, 0)),
        ),
        compiler_params=pltpu.CompilerParams(vmem_limit_bytes=40 * 2**20),
        cost_estimate=pl.CostEstimate(flops=2**31, bytes_accessed=2**22, transcendentals=2**21),
        name="query_part",
    )(scal, asked, near, far, near, far, after)


def merge_kernel(parts, out):
    heads = out.shape[1] // DH

    def stat(at, a):
        lane = heads * DH + at * heads + a
        return parts[:, :, lane : lane + 1]

    for a in range(heads):
        top = stat(0, a) + stat(1, a) + stat(2, a)
        total = stat(3, a) + stat(4, a) + stat(5, a)
        best = jnp.max(top, axis=0, keepdims=True)
        scale = jnp.exp2(top - best)
        total_all = jnp.sum(total * scale, axis=0)
        scale = scale * jnp.exp2(stat(6, a))
        summed = jnp.sum(parts[:, :, a * DH : (a + 1) * DH] * scale, axis=0)
        out[:, a * DH : (a + 1) * DH] = (summed / total_all).astype(out.dtype)


def merge_parts(parts):
    n, rows, cols = parts.shape
    return pl.pallas_call(
        merge_kernel,
        out_shape=jax.ShapeDtypeStruct((rows, cols - DH), jnp.bfloat16),
        compiler_params=pltpu.CompilerParams(vmem_limit_bytes=40 * 2**20),
        cost_estimate=pl.CostEstimate(flops=2**20, bytes_accessed=2**21, transcendentals=2**10),
        name="merge_parts",
    )(parts)


def context_kernel(shards, scal, query, *refs):
    keys, values, out, value = refs[:4], refs[4:8], refs[8], refs[9]
    own, length, hst = scal[0], scal[1], scal[2]
    rows, heads = query.shape[0], query.shape[1] // DH
    key = jnp.concatenate([r[...] for r in keys], axis=0)
    value[:, :DH] = jnp.concatenate([r[...] for r in values], axis=0)
    many = key.shape[0]

    @pl.when(pl.program_id(0) == 0)
    def _():
        value[:, DH:] = jnp.ones((many, DH), jnp.bfloat16)

    row = lax.broadcasted_iota(jnp.int32, (rows, rows), 0)
    diagonal = lax.broadcasted_iota(jnp.int32, (rows, rows), 1) <= row
    dropped = [jnp.where(scal[3 + j] < own, 0.0, NEG) for j in range(1, shards)]
    bias = [jnp.full((1, rows), d, jnp.float32) for d in dropped]
    front = many - shards * rows
    bias = jnp.concatenate(bias + [jnp.full((1, front), jnp.where(hst > 0, 0.0, NEG), jnp.float32)], axis=1)
    live = own * rows + row < length
    for a in range(heads):
        column = slice(a * DH, (a + 1) * DH)
        score = lax.dot_general(
            query[:, column], key, (((1,), (1,)), ((), ())), preferred_element_type=jnp.float32
        )
        score = jnp.concatenate(
            [jnp.where(diagonal, score[:, :rows], NEG), score[:, rows:] + bias], axis=1
        )
        top = jnp.max(score, axis=1, keepdims=True)
        weight = jnp.exp2((score - top) * EXP2_SCALE).astype(jnp.bfloat16)
        summed = jnp.dot(weight, value[...], preferred_element_type=jnp.float32)
        out[:, column] = jnp.where(live, summed[:, :DH] / summed[:, DH:], 0.0).astype(out.dtype)


def context_part(scal, query, parts, shards):
    rows, cols = query.shape
    kv_heads = parts[0].shape[1] // (2 * DH)
    group = cols // kv_heads

    def specs(offset):
        return [pl.BlockSpec((p.shape[0], DH), lambda g, s: (0, g + offset)) for p in parts]

    wide = pl.BlockSpec((rows, group), lambda g, s: (0, g))
    return pl.pallas_call(
        functools.partial(context_kernel, shards),
        out_shape=jax.ShapeDtypeStruct((rows, cols), jnp.bfloat16),
        grid_spec=pltpu.PrefetchScalarGridSpec(
            num_scalar_prefetch=1,
            grid=(kv_heads,),
            in_specs=[wide] + specs(0) + specs(kv_heads),
            out_specs=wide,
            scratch_shapes=[pltpu.VMEM((sum(p.shape[0] for p in parts), 2 * DH), jnp.bfloat16)],
        ),
        compiler_params=pltpu.CompilerParams(vmem_limit_bytes=48 * 2**20),
        cost_estimate=pl.CostEstimate(flops=2**34, bytes_accessed=2**23, transcendentals=2**24),
        name="context_part",
    )(scal, query, *parts, *parts)


def per_device(n_hst, n_head, ny, ctx_query, ctx_key, ctx_value, requests, lengths, owner):
    hst, head = lax.axis_index("hst"), lax.axis_index("head")
    chips = n_head // CORES
    pieces = requests[0].reshape(n_hst, -1, requests.shape[2])
    scattered = lax.all_to_all(pieces, "hst", 0, 0)
    piece = lax.dynamic_index_in_dim(scattered, owner[0], 0, False)
    asked = lax.all_to_all(jnp.broadcast_to(piece[None], pieces.shape), "hst", 0, 0)
    asked = asked.reshape(requests.shape[1:])
    kv = jnp.concatenate([ctx_key, ctx_value], axis=1)
    near, far = spread_over_group(kv, chips)
    anchor = spread_anchor(kv, hst, head, n_hst, n_head, ny)
    near_anchor, far_anchor = spread_over_group(anchor, chips)
    x, core = head // CORES, head % CORES
    places = [((x - step) % chips) * CORES + c for c in (core, 1 - core) for step in range(chips)]
    scal = jnp.stack([head, lengths[0], hst] + places).astype(jnp.int32)
    part = query_part(scal, asked, near, far, n_head, anchor).astype(jnp.float16)
    parts = lax.all_to_all(part.reshape(n_hst, -1, part.shape[1]), "hst", 0, 0)
    done = merge_parts(parts.astype(jnp.float32))
    query_out = lax.all_to_all(jnp.broadcast_to(done[None], (n_hst,) + done.shape), "hst", 0, 0)
    context_out = context_part(scal, ctx_query, [near, far, near_anchor, far_anchor], n_head)
    return context_out, query_out.reshape(requests.shape[1:])


def solution(mesh):
    placed = (
        P(("hst", "head"), None),
        P(("hst", "head"), None),
        P(("hst", "head"), None),
        P("hst", None, "head"),
        P("hst"),
        P(),
    )
    return jax.shard_map(
        functools.partial(per_device, mesh.shape["hst"], mesh.shape["head"], 4),
        mesh=mesh,
        in_specs=placed,
        out_specs=(P(("hst", "head"), None), P(None, "head")),
        check_vma=False,
    )
```

time: 173 us -> 143 us (0.83)
  starting transfers between devices: 83 us -> 66.5 us
  waiting for transfers between devices: 39.3 us -> 30.6 us
  Pallas kernels: 37.2 us -> 31.4 us
    all_to_all x1, waiting for transfers between devices: 0.01 us -> 12.6 us  [per_device(): parts = lax.all_to_all(part.reshape(n_hst, -1, part.shape[1]), 'hst', 0, 0)]
    ppermute x22 -> x16, waiting for transfers between devices: 30 us -> 18 us  [the longest x3 9.76 us: spread_anchor(): lax.ppermute(part, 'hst', [(k * ny, k * ny + to) for k in groups])]
    ppermute x22 -> x16, starting transfers between devices: 47.3 us -> 35.4 us  [the longest x4 14.6 us: send(): return lax.ppermute(x, 'hst', [(a * ny, b * ny) for a, b in pairs])]
    all_to_all x1, waiting for transfers between devices: 9.32 us -> 0.01 us  [per_device(): scattered = lax.all_to_all(pieces, 'hst', 0, 0)]
    pallas_call x2, Pallas kernels: 36.3 us -> 29 us  [the longest x1 22.8 us: context_part(): pl.pallas_call(functools.partial(context_kernel, shards), out_shape=jax.S...]
    all_to_all x1, starting transfers between devices: 13.4 us -> 6.54 us  [per_device(): lax.all_to_all(jnp.broadcast_to(done[None], (n_hst,) + done.shape), 'hst'...]
    all_to_all x1, starting transfers between devices: 4.97 us -> 10.9 us  [per_device(): parts = lax.all_to_all(part.reshape(n_hst, -1, part.shape[1]), 'hst', 0, 0)]
    all_to_all x1, starting transfers between devices: 12 us -> 8.72 us  [per_device(): scattered = lax.all_to_all(pieces, 'hst', 0, 0)]
  transfers between devices with their start and end apart: 26 -> 20, of which waited for: 7 -> 5; matrix products, arithmetic and copies ran while one was open for 4% -> 4% of each run, Pallas kernels for 22% -> 22%
where the time goes in v2:
time: 143 us; the launch traced here: 140 us
  starting transfers between devices  66.5 us (47%)
  Pallas kernels  31.4 us (22%)
  waiting for transfers between devices  30.6 us (21%)
  local copies, waits for them, and re-layouts  6.15 us (4%)
  other arithmetic  3.87 us (3%)
  between operations  1.65 us (1%)
    pallas_call x1, Pallas kernels, context_part(): pl.pallas_call(functools.partial(context_kernel, shards), out_shape=jax.S...  22.8 us
    ppermute x4, starting transfers between devices, send(): return lax.ppermute(x, 'hst', [(a * ny, b * ny) for a, b in pairs])  14.6 us
    all_to_all x1, waiting for transfers between devices, per_device(): parts = lax.all_to_all(part.reshape(n_hst, -1, part.shape[1]), 'hst', 0, 0)  12.6 us
    all_to_all x1, starting transfers between devices, per_device(): parts = lax.all_to_all(part.reshape(n_hst, -1, part.shape[1]), 'hst', 0, 0)  10.9 us
    ppermute x3, waiting for transfers between devices, spread_anchor(): lax.ppermute(part, 'hst', [(k * ny, k * ny + to) for k in groups])  9.76 us
    all_to_all x1, starting transfers between devices, per_device(): scattered = lax.all_to_all(pieces, 'hst', 0, 0)  8.72 us
    ppermute x6, waiting for transfers between devices, spread_over_group(): lax.ppermute(shard, 'head', [(i, (i + step * CORES) % size) for i in rang...  8.23 us
    ppermute x3, starting transfers between devices, spread_anchor(): lax.ppermute(part, 'hst', [(k * ny, k * ny + to) for k in groups])  7.74 us
  transfers between devices with their start and end apart: 20, of which 5 were waited for; matrix products, arithmetic and copies ran while one was open for 4% of the time, Pallas kernels for 22%

profile of v2, /device:TPU:1, one launch (start us, length us, event | category | flops | bytes accessed | tf_op | source)
XLA Modules:
  0.0 140.2 jit_solution(12865902600622404678)
XLA Ops:
  2.6 5.5 %collective-permute-start.4 = (bf16[64,2048]{1,0:T(8,128)(2,1)S(1)}, bf16[64,2048]{1,0:T(8,128)(2,1)S(1)}, u32[]{:S(2)}, u32[]{:S(2)}) collective-permute-start(bf16[64,2048]{1,0:T(8,128)(2,1)S(1)} %slice.13), channel_id=1, source_target_pairs={{0,4},{1,5},{2,6},{3,7}} | collective-permute-start | bytes 786440 | tf_op jit(solution)/shard_map/ppermute | solution.py:29
  8.2 2.1 %collective-permute-start.1 = (bf16[128,2048]{1,0:T(8,128)(2,1)S(1)}, bf16[128,2048]{1,0:T(8,128)(2,1)}, u32[]{:S(2)}, u32[]{:S(2)}) collective-permute-start(bf16[128,2048]{1,0:T(8,128)(2,1)S(1)} %constant_dynamic-update-slice_fusion), channel_id=1, source_target_pairs={{0,4},{1,5},{2,6},{3,7},{4,0},{5,1},{6,2},{7,3},{8,12},{9,13},{10,... | collective-permute-start | bytes 1572872 | tf_op jit(solution)/shard_map/ppermute | solution.py:19
  10.3 8.7 %all-to-all-start = ((bf16[32,8,1024]{2,1,0:T(8,128)(2,1)}), bf16[32,8,1024]{2,1,0:T(8,128)(2,1)S(1)}, u32[]{:S(2)}, u32[]{:S(2)}) async-start(bf16[32,8,1024]{2,1,0:T(8,128)(2,1)} %bitcast.21), calls=%async_computation | async-start | bytes 1048576 | tf_op jit(solution)/shard_map/all_to_all | solution.py:201
  19.1 5.7 %collective-permute-start.5 = (bf16[64,2048]{1,0:T(8,128)(2,1)S(1)}, bf16[64,2048]{1,0:T(8,128)(2,1)}, u32[]{:S(2)}, u32[]{:S(2)}) collective-permute-start(bf16[64,2048]{1,0:T(8,128)(2,1)S(1)} %slice_select_fusion), channel_id=1, source_target_pairs={{0,96},{1,97},{2,98},{3,99},{4,100},{5,101},{6,102},{7,103}} | collective-permute-start | bytes 786440 | tf_op jit(solution)/shard_map/ppermute | solution.py:34
  24.7 2.6 %collective-permute-start.6 = (bf16[64,2048]{1,0:T(8,128)(2,1)S(1)}, bf16[64,2048]{1,0:T(8,128)(2,1)}, u32[]{:S(2)}, u32[]{:S(2)}) collective-permute-start(bf16[64,2048]{1,0:T(8,128)(2,1)S(1)} %slice_select_fusion), channel_id=1, source_target_pairs={{0,160},{1,161},{2,162},{3,163},{4,164},{5,165},{6,166},{7,167}} | collective-permute-start | bytes 786440 | tf_op jit(solution)/shard_map/ppermute | solution.py:34
  27.3 8.2 %collective-permute-done = bf16[128,2048]{1,0:T(8,128)(2,1)} collective-permute-done((bf16[128,2048]{1,0:T(8,128)(2,1)S(1)}, bf16[128,2048]{1,0:T(8,128)(2,1)}, u32[]{:S(2)}, u32[]{:S(2)}) %collective-permute-start) | collective-permute-done | bytes 524320 | tf_op jit(solution)/shard_map/ppermute | solution.py:19
  37.1 1.6 %collective-permute-start.3 = (bf16[512,2048]{1,0:T(8,128)(2,1)S(1)}, bf16[512,2048]{1,0:T(8,128)(2,1)}, u32[]{:S(2)}, u32[]{:S(2)}) collective-permute-start(bf16[512,2048]{1,0:T(8,128)(2,1)S(1)} %pad_maximum_fusion.refs_0_.refs_4_.near_key.near_value), channel_id=1, source_target_pairs={{0,1},{1,0},{2,3},{3,2},{4,5},{5,4},{6,7},{7,6},{8,9},{9,8},{10,11... | collective-permute-start | bytes 6291464 | tf_op jit(solution)/shard_map/ppermute | solution.py:23
  38.8 2.0 %collective-permute-start.7 = (bf16[64,2048]{1,0:T(8,128)(2,1)S(1)}, bf16[64,2048]{1,0:T(8,128)(2,1)}, u32[]{:S(2)}, u32[]{:S(2)}) collective-permute-start(bf16[64,2048]{1,0:T(8,128)(2,1)S(1)} %select_select_fusion.2), channel_id=1, source_target_pairs={{0,32},{96,128},{160,192},{1,33},{97,129},{161,193},{2,34},{98,130... | collective-permute-start | bytes 786440 | tf_op jit(solution)/shard_map/ppermute | solution.py:34
  40.8 4.3 %collective-permute-start.8 = (bf16[64,2048]{1,0:T(8,128)(2,1)S(1)}, bf16[64,2048]{1,0:T(8,128)(2,1)}, u32[]{:S(2)}, u32[]{:S(2)}) collective-permute-start(bf16[64,2048]{1,0:T(8,128)(2,1)S(1)} %select_select_fusion.2), channel_id=1, source_target_pairs={{0,224},{96,64},{1,225},{97,65},{2,226},{98,66},{3,227},{99,67},{4... | collective-permute-start | bytes 786440 | tf_op jit(solution)/shard_map/ppermute | solution.py:34
  46.1 5.0 %all-to-all-start.1 = ((bf16[32,8,1024]{2,1,0:T(8,128)(2,1)}), bf16[32,8,1024]{2,1,0:T(8,128)(2,1)S(1)}, u32[]{:S(2)}, u32[]{:S(2)}) async-start(bf16[32,8,1024]{2,1,0:T(8,128)(2,1)} %broadcast_in_dim.7), calls=%async_computation.1 | async-start | bytes 1048576 | tf_op jit(solution)/shard_map/all_to_all | solution.py:203
  51.2 3.1 %collective-permute-start.9 = (bf16[64,2048]{1,0:T(8,128)(2,1)S(1)}, bf16[64,2048]{1,0:T(8,128)(2,1)S(1)}, u32[]{:S(2)}, u32[]{:S(2)}) collective-permute-start(bf16[64,2048]{1,0:T(8,128)(2,1)S(1)} %select_select_fusion.1), channel_id=1, source_target_pairs={{0,8},{32,40},{64,72},{96,104},{128,136},{160,168},{192,200},{224,... | collective-permute-start | bytes 786440 | tf_op jit(solution)/shard_map/ppermute | solution.py:42
  54.3 2.6 %collective-permute-start.10 = (bf16[64,2048]{1,0:T(8,128)(2,1)S(1)}, bf16[64,2048]{1,0:T(8,128)(2,1)}, u32[]{:S(2)}, u32[]{:S(2)}) collective-permute-start(bf16[64,2048]{1,0:T(8,128)(2,1)S(1)} %select_select_fusion.1), channel_id=1, source_target_pairs={{0,24},{32,56},{64,88},{96,120},{128,152},{160,184},{192,216},{224... | collective-permute-start | bytes 786440 | tf_op jit(solution)/shard_map/ppermute | solution.py:42
  56.9 2.0 %collective-permute-start.11 = (bf16[64,2048]{1,0:T(8,128)(2,1)S(1)}, bf16[64,2048]{1,0:T(8,128)(2,1)}, u32[]{:S(2)}, u32[]{:S(2)}) collective-permute-start(bf16[64,2048]{1,0:T(8,128)(2,1)S(1)} %select_select_fusion.1), channel_id=1, source_target_pairs={{0,16},{32,48},{64,80},{96,112},{128,144},{160,176},{192,208},{224... | collective-permute-start | bytes 786440 | tf_op jit(solution)/shard_map/ppermute | solution.py:42
  59.7 2.8 %collective-permute-done.9 = bf16[64,2048]{1,0:T(8,128)(2,1)S(1)} collective-permute-done((bf16[64,2048]{1,0:T(8,128)(2,1)S(1)}, bf16[64,2048]{1,0:T(8,128)(2,1)S(1)}, u32[]{:S(2)}, u32[]{:S(2)}) %collective-permute-start.9) | collective-permute-done | bytes 262176 | tf_op jit(solution)/shard_map/ppermute | solution.py:42
  62.5 2.8 %collective-permute-done.10 = bf16[64,2048]{1,0:T(8,128)(2,1)} collective-permute-done((bf16[64,2048]{1,0:T(8,128)(2,1)S(1)}, bf16[64,2048]{1,0:T(8,128)(2,1)}, u32[]{:S(2)}, u32[]{:S(2)}) %collective-permute-start.10) | collective-permute-done | bytes 262176 | tf_op jit(solution)/shard_map/ppermute | solution.py:42
  65.3 4.1 %collective-permute-done.11 = bf16[64,2048]{1,0:T(8,128)(2,1)} collective-permute-done((bf16[64,2048]{1,0:T(8,128)(2,1)S(1)}, bf16[64,2048]{1,0:T(8,128)(2,1)}, u32[]{:S(2)}, u32[]{:S(2)}) %collective-permute-start.11) | collective-permute-done | bytes 262176 | tf_op jit(solution)/shard_map/ppermute | solution.py:42
  71.1 6.2 %query_part.1 = f32[256,1152]{1,0:T(8,128)S(1)} custom-call(s32[11]{0:T(128)S(1)} %stack.43.scal, bf16[256,1024]{1,0:T(8,128)(2,1)S(1)} %bitcast.19, bf16[512,2048]{1,0:T(8,128)(2,1)S(1)} %pad_maximum_fusion.refs_0_.refs_4_.near_key.near_value, bf16[512,2048]{1,0:T(8,128)(2,1)} %collective-permute-done.3.refs_1_.refs_5_.far_key.far_value, ...), custom_call_target="tpu_custom_call" | custom-call | flops 2147483648 | bytes 4194304 | tf_op jit(solution)/shard_map/query_part/pallas_call | solution.py:88
  78.2 10.9 %all-to-all-start.2 = ((f16[32,8,1152]{2,1,0:T(8,128)(2,1)}), f16[32,8,1152]{2,1,0:T(8,128)(2,1)S(1)}, u32[]{:S(2)}, u32[]{:S(2)}) async-start(f16[32,8,1152]{2,1,0:T(8,128)(2,1)} %convert_bitcast_fusion), calls=%async_computation.2 | async-start | bytes 1179648 | tf_op jit(solution)/shard_map/all_to_all | solution.py:213
  90.3 2.2 %collective-permute-start.15 = (bf16[256,2048]{1,0:T(8,128)(2,1)S(1)}, bf16[256,2048]{1,0:T(8,128)(2,1)S(1)}, u32[]{:S(2)}, u32[]{:S(2)}) collective-permute-start(bf16[256,2048]{1,0:T(8,128)(2,1)S(1)} %pad_maximum_fusion.1.refs_2_.refs_6_), channel_id=1, source_target_pairs={{0,1},{1,0},{2,3},{3,2},{4,5},{5,4},{6,7},{7,6},{8,9},{9,8},{10,11... | collective-permute-start | bytes 3145736 | tf_op jit(solution)/shard_map/ppermute | solution.py:23
  92.5 12.6 %all-to-all-done.2 = f16[32,8,1152]{2,1,0:T(8,128)(2,1)S(1)} async-done(((f16[32,8,1152]{2,1,0:T(8,128)(2,1)}), f16[32,8,1152]{2,1,0:T(8,128)(2,1)S(1)}, u32[]{:S(2)}, u32[]{:S(2)}) %all-to-all-start.2) | async-done | bytes 589856 | tf_op jit(solution)/shard_map/all_to_all | solution.py:213
  105.2 2.4 %merge_parts.1 = bf16[8,1024]{1,0:T(8,128)(2,1)S(1)} custom-call(f32[32,8,1152]{2,1,0:T(8,128)S(1)} %convert_element_type.7.parts), custom_call_target="tpu_custom_call" | custom-call | flops 1048576 | bytes 2097152 | tf_op jit(solution)/shard_map/merge_parts/pallas_call | solution.py:130
  108.5 6.5 %all-to-all-start.3 = ((bf16[32,8,1024]{2,1,0:T(8,128)(2,1)}), bf16[32,8,1024]{2,1,0:T(8,128)(2,1)S(1)}, u32[]{:S(2)}, u32[]{:S(2)}) async-start(bf16[32,8,1024]{2,1,0:T(8,128)(2,1)} %broadcast_in_dim.16), calls=%async_computation.3 | async-start | bytes 1048576 | tf_op jit(solution)/shard_map/all_to_all | solution.py:215
  115.1 1.6 %copy-done.1 = bf16[128,8192]{1,0:T(8,128)(2,1)S(1)} copy-done((bf16[128,8192]{1,0:T(8,128)(2,1)S(1)}, bf16[128,8192]{1,0:T(8,128)(2,1)}, u32[]{:S(2)}) %copy-start.1) | copy-done | bytes 2097176
  116.6 22.8 %context_part.1 = bf16[128,8192]{1,0:T(8,128)(2,1)} custom-call(s32[11]{0:T(128)S(1)} %stack.43.scal, bf16[128,8192]{1,0:T(8,128)(2,1)S(1)} %copy-done.1, bf16[512,2048]{1,0:T(8,128)(2,1)} %copy-done, bf16[512,2048]{1,0:T(8,128)(2,1)} %collective-permute-done.3.refs_1_.refs_5_.far_key.far_value, bf16[256,2048]{1,0:T(8,128)(2,1)S(1)} %pad_maximum_fusion.1.refs_2_.refs_6_, ...), custom_call_target="tpu_custom_call" | custom-call | flops 17179869184 | bytes 8388608 | tf_op jit(solution)/shard_map/context_part/pallas_call | solution.py:181
  (41 shorter events, 10.1 us)
Async XLA Ops:
  2.6 16.4 %collective-permute-start.4 = (bf16[64,2048]{1,0:T(8,128)(2,1)S(1)}, bf16[64,2048]{1,0:T(8,128)(2,1)S(1)}, u32[]{:S(2)}, u32[]{:S(2)}) collective-permute-start(bf16[64,2048]{1,0:T(8,128)(2,1)S(1)} %slice.13), channel_id=1, source_target_pairs={{0,4},{1,5},{2,6},{3,7}} | collective-permute-start | bytes 786440 | tf_op jit(solution)/shard_map/ppermute | solution.py:29
  8.1 19.2 %collective-permute-start.2 = (bf16[128,2048]{1,0:T(8,128)(2,1)S(1)}, bf16[128,2048]{1,0:T(8,128)(2,1)}, u32[]{:S(2)}, u32[]{:S(2)}) collective-permute-start(bf16[128,2048]{1,0:T(8,128)(2,1)S(1)} %constant_dynamic-update-slice_fusion), channel_id=1, source_target_pairs={{0,6},{1,7},{2,0},{3,1},{4,2},{5,3},{6,4},{7,5},{8,14},{9,15},{10,... | collective-permute-start | bytes 1572872 | tf_op jit(solution)/shard_map/ppermute | solution.py:19
  8.2 19.1 %collective-permute-start.1 = (bf16[128,2048]{1,0:T(8,128)(2,1)S(1)}, bf16[128,2048]{1,0:T(8,128)(2,1)}, u32[]{:S(2)}, u32[]{:S(2)}) collective-permute-start(bf16[128,2048]{1,0:T(8,128)(2,1)S(1)} %constant_dynamic-update-slice_fusion), channel_id=1, source_target_pairs={{0,4},{1,5},{2,6},{3,7},{4,0},{5,1},{6,2},{7,3},{8,12},{9,13},{10,... | collective-permute-start | bytes 1572872 | tf_op jit(solution)/shard_map/ppermute | solution.py:19
  10.3 25.3 %collective-permute-start = (bf16[128,2048]{1,0:T(8,128)(2,1)S(1)}, bf16[128,2048]{1,0:T(8,128)(2,1)}, u32[]{:S(2)}, u32[]{:S(2)}) collective-permute-start(bf16[128,2048]{1,0:T(8,128)(2,1)S(1)} %constant_dynamic-update-slice_fusion), channel_id=1, source_target_pairs={{0,2},{1,3},{2,4},{3,5},{4,6},{5,7},{6,0},{7,1},{8,10},{9,11},{10,... | collective-permute-start | bytes 1572872 | tf_op jit(solution)/shard_map/ppermute | solution.py:19
  10.3 34.9 %all-to-all-start = ((bf16[32,8,1024]{2,1,0:T(8,128)(2,1)}), bf16[32,8,1024]{2,1,0:T(8,128)(2,1)S(1)}, u32[]{:S(2)}, u32[]{:S(2)}) async-start(bf16[32,8,1024]{2,1,0:T(8,128)(2,1)} %bitcast.21), calls=%async_computation | async-start | bytes 1048576 | tf_op jit(solution)/shard_map/all_to_all | solution.py:201
  19.1 26.0 %copy-start.2 = (s32[32]{0:T(128)S(1)}, s32[32]{0:T(128)}, u32[]{:S(2)}) copy-start(s32[32]{0:T(128)} %param.11) | copy-start | bytes 388
  19.1 19.6 %collective-permute-start.5 = (bf16[64,2048]{1,0:T(8,128)(2,1)S(1)}, bf16[64,2048]{1,0:T(8,128)(2,1)}, u32[]{:S(2)}, u32[]{:S(2)}) collective-permute-start(bf16[64,2048]{1,0:T(8,128)(2,1)S(1)} %slice_select_fusion), channel_id=1, source_target_pairs={{0,96},{1,97},{2,98},{3,99},{4,100},{5,101},{6,102},{7,103}} | collective-permute-start | bytes 786440 | tf_op jit(solution)/shard_map/ppermute | solution.py:34
  24.7 14.0 %collective-permute-start.6 = (bf16[64,2048]{1,0:T(8,128)(2,1)S(1)}, bf16[64,2048]{1,0:T(8,128)(2,1)}, u32[]{:S(2)}, u32[]{:S(2)}) collective-permute-start(bf16[64,2048]{1,0:T(8,128)(2,1)S(1)} %slice_select_fusion), channel_id=1, source_target_pairs={{0,160},{1,161},{2,162},{3,163},{4,164},{5,165},{6,166},{7,167}} | collective-permute-start | bytes 786440 | tf_op jit(solution)/shard_map/ppermute | solution.py:34
  37.1 34.0 %copy-start = (bf16[512,2048]{1,0:T(8,128)(2,1)}, bf16[512,2048]{1,0:T(8,128)(2,1)S(1)}, u32[]{:S(2)}) copy-start(bf16[512,2048]{1,0:T(8,128)(2,1)S(1)} %pad_maximum_fusion.refs_0_.refs_4_.near_key.near_value) | copy-start | bytes 6291460
  37.1 34.0 %collective-permute-start.3 = (bf16[512,2048]{1,0:T(8,128)(2,1)S(1)}, bf16[512,2048]{1,0:T(8,128)(2,1)}, u32[]{:S(2)}, u32[]{:S(2)}) collective-permute-start(bf16[512,2048]{1,0:T(8,128)(2,1)S(1)} %pad_maximum_fusion.refs_0_.refs_4_.near_key.near_value), channel_id=1, source_target_pairs={{0,1},{1,0},{2,3},{3,2},{4,5},{5,4},{6,7},{7,6},{8,9},{9,8},{10,11... | collective-permute-start | bytes 6291464 | tf_op jit(solution)/shard_map/ppermute | solution.py:23
  38.8 12.3 %collective-permute-start.7 = (bf16[64,2048]{1,0:T(8,128)(2,1)S(1)}, bf16[64,2048]{1,0:T(8,128)(2,1)}, u32[]{:S(2)}, u32[]{:S(2)}) collective-permute-start(bf16[64,2048]{1,0:T(8,128)(2,1)S(1)} %select_select_fusion.2), channel_id=1, source_target_pairs={{0,32},{96,128},{160,192},{1,33},{97,129},{161,193},{2,34},{98,130... | collective-permute-start | bytes 786440 | tf_op jit(solution)/shard_map/ppermute | solution.py:34
  40.8 10.3 %collective-permute-start.8 = (bf16[64,2048]{1,0:T(8,128)(2,1)S(1)}, bf16[64,2048]{1,0:T(8,128)(2,1)}, u32[]{:S(2)}, u32[]{:S(2)}) collective-permute-start(bf16[64,2048]{1,0:T(8,128)(2,1)S(1)} %select_select_fusion.2), channel_id=1, source_target_pairs={{0,224},{96,64},{1,225},{97,65},{2,226},{98,66},{3,227},{99,67},{4... | collective-permute-start | bytes 786440 | tf_op jit(solution)/shard_map/ppermute | solution.py:34
  46.1 25.0 %all-to-all-start.1 = ((bf16[32,8,1024]{2,1,0:T(8,128)(2,1)}), bf16[32,8,1024]{2,1,0:T(8,128)(2,1)S(1)}, u32[]{:S(2)}, u32[]{:S(2)}) async-start(bf16[32,8,1024]{2,1,0:T(8,128)(2,1)} %broadcast_in_dim.7), calls=%async_computation.1 | async-start | bytes 1048576 | tf_op jit(solution)/shard_map/all_to_all | solution.py:203
  51.2 11.3 %collective-permute-start.9 = (bf16[64,2048]{1,0:T(8,128)(2,1)S(1)}, bf16[64,2048]{1,0:T(8,128)(2,1)S(1)}, u32[]{:S(2)}, u32[]{:S(2)}) collective-permute-start(bf16[64,2048]{1,0:T(8,128)(2,1)S(1)} %select_select_fusion.1), channel_id=1, source_target_pairs={{0,8},{32,40},{64,72},{96,104},{128,136},{160,168},{192,200},{224,... | collective-permute-start | bytes 786440 | tf_op jit(solution)/shard_map/ppermute | solution.py:42
  54.3 11.0 %collective-permute-start.10 = (bf16[64,2048]{1,0:T(8,128)(2,1)S(1)}, bf16[64,2048]{1,0:T(8,128)(2,1)}, u32[]{:S(2)}, u32[]{:S(2)}) collective-permute-start(bf16[64,2048]{1,0:T(8,128)(2,1)S(1)} %select_select_fusion.1), channel_id=1, source_target_pairs={{0,24},{32,56},{64,88},{96,120},{128,152},{160,184},{192,216},{224... | collective-permute-start | bytes 786440 | tf_op jit(solution)/shard_map/ppermute | solution.py:42
  56.9 12.5 %collective-permute-start.11 = (bf16[64,2048]{1,0:T(8,128)(2,1)S(1)}, bf16[64,2048]{1,0:T(8,128)(2,1)}, u32[]{:S(2)}, u32[]{:S(2)}) collective-permute-start(bf16[64,2048]{1,0:T(8,128)(2,1)S(1)} %select_select_fusion.1), channel_id=1, source_target_pairs={{0,16},{32,48},{64,80},{96,112},{128,144},{160,176},{192,208},{224... | collective-permute-start | bytes 786440 | tf_op jit(solution)/shard_map/ppermute | solution.py:42
  69.5 19.6 %collective-permute-start.14 = (bf16[64,2048]{1,0:T(8,128)(2,1)S(1)}, bf16[64,2048]{1,0:T(8,128)(2,1)}, u32[]{:S(2)}, u32[]{:S(2)}) collective-permute-start(bf16[64,2048]{1,0:T(8,128)(2,1)S(1)} %select_select_fusion.after), channel_id=1, source_target_pairs={{0,6},{1,7},{2,0},{3,1},{4,2},{5,3},{6,4},{7,5},{8,14},{9,15},{10,... | collective-permute-start | bytes 786440 | tf_op jit(solution)/shard_map/ppermute | solution.py:19
  69.6 19.5 %collective-permute-start.13 = (bf16[64,2048]{1,0:T(8,128)(2,1)S(1)}, bf16[64,2048]{1,0:T(8,128)(2,1)}, u32[]{:S(2)}, u32[]{:S(2)}) collective-permute-start(bf16[64,2048]{1,0:T(8,128)(2,1)S(1)} %select_select_fusion.after), channel_id=1, source_target_pairs={{0,4},{1,5},{2,6},{3,7},{4,0},{5,1},{6,2},{7,3},{8,12},{9,13},{10,... | collective-permute-start | bytes 786440 | tf_op jit(solution)/shard_map/ppermute | solution.py:19
  70.2 18.9 %collective-permute-start.12 = (bf16[64,2048]{1,0:T(8,128)(2,1)S(1)}, bf16[64,2048]{1,0:T(8,128)(2,1)}, u32[]{:S(2)}, u32[]{:S(2)}) collective-permute-start(bf16[64,2048]{1,0:T(8,128)(2,1)S(1)} %select_select_fusion.after), channel_id=1, source_target_pairs={{0,2},{1,3},{2,4},{3,5},{4,6},{5,7},{6,0},{7,1},{8,10},{9,11},{10,... | collective-permute-start | bytes 786440 | tf_op jit(solution)/shard_map/ppermute | solution.py:19
  78.2 26.9 %all-to-all-start.2 = ((f16[32,8,1152]{2,1,0:T(8,128)(2,1)}), f16[32,8,1152]{2,1,0:T(8,128)(2,1)S(1)}, u32[]{:S(2)}, u32[]{:S(2)}) async-start(f16[32,8,1152]{2,1,0:T(8,128)(2,1)} %convert_bitcast_fusion), calls=%async_computation.2 | async-start | bytes 1179648 | tf_op jit(solution)/shard_map/all_to_all | solution.py:213
  90.3 24.7 %collective-permute-start.15 = (bf16[256,2048]{1,0:T(8,128)(2,1)S(1)}, bf16[256,2048]{1,0:T(8,128)(2,1)S(1)}, u32[]{:S(2)}, u32[]{:S(2)}) collective-permute-start(bf16[256,2048]{1,0:T(8,128)(2,1)S(1)} %pad_maximum_fusion.1.refs_2_.refs_6_), channel_id=1, source_target_pairs={{0,1},{1,0},{2,3},{3,2},{4,5},{5,4},{6,7},{7,6},{8,9},{9,8},{10,11... | collective-permute-start | bytes 3145736 | tf_op jit(solution)/shard_map/ppermute | solution.py:23
  108.5 30.9 %all-to-all-start.3 = ((bf16[32,8,1024]{2,1,0:T(8,128)(2,1)}), bf16[32,8,1024]{2,1,0:T(8,128)(2,1)S(1)}, u32[]{:S(2)}, u32[]{:S(2)}) async-start(bf16[32,8,1024]{2,1,0:T(8,128)(2,1)} %broadcast_in_dim.16), calls=%async_computation.3 | async-start | bytes 1048576 | tf_op jit(solution)/shard_map/all_to_all | solution.py:215
  115.0 1.6 %copy-start.1 = (bf16[128,8192]{1,0:T(8,128)(2,1)S(1)}, bf16[128,8192]{1,0:T(8,128)(2,1)}, u32[]{:S(2)}) copy-start(bf16[128,8192]{1,0:T(8,128)(2,1)} %query.1) | copy-start | bytes 6291460

commit v3 on v2

--- a/solution.py
+++ b/solution.py
@@ -52,54 +52,62 @@
     return parts
 
 
-def query_kernel(shards, scal, asked, near_key, far_key, near_value, far_value, after, out):
+def query_kernel(shards, scal, asked, near_key, far_key, near_value, far_value, after, out, value):
     length = scal[1]
-    rows, heads = asked.shape[0], asked.shape[1] // DH
+    rows, cols = asked.shape
+    heads = cols // DH
     key = jnp.concatenate([near_key[...], far_key[...]], axis=0)
-    value = jnp.concatenate([near_value[...], far_value[...]], axis=0)
-    width = key.shape[0] // shards
+    many = key.shape[0]
+    value[:, :DH] = jnp.concatenate([near_value[...], far_value[...]], axis=0)
+    value[:, DH:] = jnp.ones((many, DH), jnp.bfloat16)
+    width = many // shards
     lane = lax.broadcasted_iota(jnp.int32, (1, width), 1)
     keep = jnp.concatenate([lane + scal[3 + j] * width for j in range(shards)], axis=1) < length
-    column = lax.broadcasted_iota(jnp.int32, (rows, DH), 1)
-    stats = jnp.zeros((rows, DH), jnp.float32)
-    for a in range(heads):
-        query = asked[:, a * DH : (a + 1) * DH]
-        score = lax.dot_general(query, key, (((1,), (1,)), ((), ())), preferred_element_type=jnp.float32)
-        score = jnp.where(keep, score, NEG)
-        top = jnp.max(score, axis=1, keepdims=True)
-        weight = jnp.exp2((score - top) * EXP2_SCALE)
-        total = jnp.sum(weight, axis=1, keepdims=True)
-        summed = jnp.dot(weight.astype(jnp.bfloat16), value, preferred_element_type=jnp.float32)
-        reach = jnp.max(jnp.abs(summed), axis=1, keepdims=True)
-        power = jnp.ceil(jnp.log2(jnp.maximum(reach, 1e-36)))
-        out[:, a * DH : (a + 1) * DH] = summed * jnp.exp2(-power)
-        values = pieces_of(top * EXP2_SCALE) + pieces_of(total) + [power]
-        for at, stat in enumerate(values):
-            stats = jnp.where(column == at * heads + a, stat, stats)
-    out[:, heads * DH :] = stats
-
-
-def query_part(scal, asked, near, far, shards, after):
+    some = 128
+    column = lax.broadcasted_iota(jnp.int32, (some, DH), 1)
+    high = out.shape[1]
+    for first in range(0, rows, some):
+        to = slice(first // high, (first + some) // high)
+        stats = jnp.zeros((some, DH), jnp.float32)
+        for a in range(heads):
+            mine = slice(a * DH, (a + 1) * DH)
+            score = lax.dot_general(
+                asked[first : first + some, mine],
+                key,
+                (((1,), (1,)), ((), ())),
+                preferred_element_type=jnp.float32,
+            )
+            score = jnp.where(keep, score, NEG)
+            top = jnp.max(score, axis=1, keepdims=True)
+            weight = jnp.exp2((score - top) * EXP2_SCALE).astype(jnp.bfloat16)
+            both = jnp.dot(weight, value[...], preferred_element_type=jnp.float32)
+            summed, total = both[:, :DH], both[:, DH:]
+            reach = jnp.max(jnp.abs(summed), axis=1, keepdims=True)
+            power = jnp.ceil(jnp.log2(jnp.maximum(reach, 1e-36)))
+            out[to, :, mine] = (summed * jnp.exp2(-power)).reshape(some // high, high, DH)
+            values = pieces_of(top * EXP2_SCALE) + pieces_of(total) + [power]
+            for at, stat in enumerate(values):
+                stats = jnp.where(column == at * heads + a, stat, stats)
+        out[to, :, cols:] = stats.reshape(some // high, high, DH)
+
+
+def query_part(scal, asked, near, far, shards, n, after):
     rows, cols = asked.shape
     width = near.shape[0]
     kv_heads = near.shape[1] // (2 * DH)
     key = pl.BlockSpec((width, DH), lambda i, s: (0, s[0]))
     value = pl.BlockSpec((width, DH), lambda i, s: (0, kv_heads + s[0]))
+    result = (n, rows // n, cols + DH)
     return pl.pallas_call(
         functools.partial(query_kernel, shards),
-        out_shape=jax.ShapeDtypeStruct((rows, cols + DH), jnp.float32),
+        out_shape=jax.ShapeDtypeStruct(result, jnp.float32),
         grid_spec=pltpu.PrefetchScalarGridSpec(
             num_scalar_prefetch=1,
             grid=(1,),
-            in_specs=[
-                pl.BlockSpec((rows, cols), lambda i, s: (0, 0)),
-                key,
-                key,
-                value,
-                value,
-                pl.BlockSpec(memory_space=pl.ANY),
-            ],
-            out_specs=pl.BlockSpec((rows, cols + DH), lambda i, s: (0, 0)),
+            in_specs=[pl.BlockSpec((rows, cols), lambda i, s: (0, 0)), key, key, value, value]
+            + [pl.BlockSpec(memory_space=pl.ANY)],
+            out_specs=pl.BlockSpec(result, lambda i, s: (0, 0, 0)),
+            scratch_shapes=[pltpu.VMEM((2 * width, 2 * DH), jnp.bfloat16)],
         ),
         compiler_params=pltpu.CompilerParams(vmem_limit_bytes=40 * 2**20),
         cost_estimate=pl.CostEstimate(flops=2**31, bytes_accessed=2**22, transcendentals=2**21),
@@ -108,7 +116,7 @@
 
 
 def merge_kernel(parts, out):
-    heads = out.shape[1] // DH
+    heads = out.shape[2] // DH
 
     def stat(at, a):
         lane = heads * DH + at * heads + a
@@ -122,14 +130,15 @@
         total_all = jnp.sum(total * scale, axis=0)
         scale = scale * jnp.exp2(stat(6, a))
         summed = jnp.sum(parts[:, :, a * DH : (a + 1) * DH] * scale, axis=0)
-        out[:, a * DH : (a + 1) * DH] = (summed / total_all).astype(out.dtype)
+        done = (summed / total_all).astype(out.dtype)
+        out[:, :, a * DH : (a + 1) * DH] = jnp.broadcast_to(done[None], (out.shape[0],) + done.shape)
 
 
 def merge_parts(parts):
     n, rows, cols = parts.shape
     return pl.pallas_call(
         merge_kernel,
-        out_shape=jax.ShapeDtypeStruct((rows, cols - DH), jnp.bfloat16),
+        out_shape=jax.ShapeDtypeStruct((n, rows, cols - DH), jnp.bfloat16),
         compiler_params=pltpu.CompilerParams(vmem_limit_bytes=40 * 2**20),
         cost_estimate=pl.CostEstimate(flops=2**20, bytes_accessed=2**21, transcendentals=2**10),
         name="merge_parts",
@@ -169,29 +178,35 @@
         out[:, column] = jnp.where(live, summed[:, :DH] / summed[:, DH:], 0.0).astype(out.dtype)
 
 
-def context_part(scal, query, parts, shards):
+def context_part(scal, query, parts, shards, first, count, before, after, flops):
     rows, cols = query.shape
     kv_heads = parts[0].shape[1] // (2 * DH)
     group = cols // kv_heads
 
     def specs(offset):
-        return [pl.BlockSpec((p.shape[0], DH), lambda g, s: (0, g + offset)) for p in parts]
-
-    wide = pl.BlockSpec((rows, group), lambda g, s: (0, g))
+        return [pl.BlockSpec((p.shape[0], DH), lambda g, s: (0, first + g + offset)) for p in parts]
+
+    wide = pl.BlockSpec((rows, group), lambda g, s: (0, first + g))
+    extra = ([] if before is None else [before]) + after
+
+    def kernel(scal, query, *refs):
+        context_kernel(shards, scal, query, *refs[: 2 * len(parts)], *refs[2 * len(parts) + len(extra) :])
+
     return pl.pallas_call(
-        functools.partial(context_kernel, shards),
+        kernel,
         out_shape=jax.ShapeDtypeStruct((rows, cols), jnp.bfloat16),
         grid_spec=pltpu.PrefetchScalarGridSpec(
             num_scalar_prefetch=1,
-            grid=(kv_heads,),
-            in_specs=[wide] + specs(0) + specs(kv_heads),
+            grid=(count,),
+            in_specs=[wide] + specs(0) + specs(kv_heads) + [pl.BlockSpec(memory_space=pl.ANY)] * len(extra),
             out_specs=wide,
             scratch_shapes=[pltpu.VMEM((sum(p.shape[0] for p in parts), 2 * DH), jnp.bfloat16)],
         ),
-        compiler_params=pltpu.CompilerParams(vmem_limit_bytes=48 * 2**20),
-        cost_estimate=pl.CostEstimate(flops=2**34, bytes_accessed=2**23, transcendentals=2**24),
+        input_output_aliases={} if before is None else {2 + 2 * len(parts): 0},
+        compiler_params=pltpu.CompilerParams(vmem_limit_bytes=62 * 2**20),
+        cost_estimate=pl.CostEstimate(flops=flops, bytes_accessed=2**10, transcendentals=0),
         name="context_part",
-    )(scal, query, *parts, *parts)
+    )(scal, query, *parts, *parts, *extra)
 
 
 def per_device(n_hst, n_head, ny, ctx_query, ctx_key, ctx_value, requests, lengths, owner):
@@ -209,11 +224,14 @@
     x, core = head // CORES, head % CORES
     places = [((x - step) % chips) * CORES + c for c in (core, 1 - core) for step in range(chips)]
     scal = jnp.stack([head, lengths[0], hst] + places).astype(jnp.int32)
-    part = query_part(scal, asked, near, far, n_head, anchor).astype(jnp.float16)
-    parts = lax.all_to_all(part.reshape(n_hst, -1, part.shape[1]), "hst", 0, 0)
-    done = merge_parts(parts.astype(jnp.float32))
-    query_out = lax.all_to_all(jnp.broadcast_to(done[None], (n_hst,) + done.shape), "hst", 0, 0)
-    context_out = context_part(scal, ctx_query, [near, far, near_anchor, far_anchor], n_head)
+    part = query_part(scal, asked, near, far, n_head, n_hst, anchor).astype(jnp.float16)
+    parts = lax.all_to_all(part, "hst", 0, 0).astype(jnp.float32)
+    kv_parts = [near, far, near_anchor, far_anchor]
+    begun = context_part(scal, ctx_query, kv_parts, n_head, 0, 2, None, [], 2**20)
+    parts, begun = lax.optimization_barrier((parts, begun))
+    done = merge_parts(parts)
+    query_out = lax.all_to_all(done, "hst", 0, 0)
+    context_out = context_part(scal, ctx_query, kv_parts, n_head, 2, n_head - 2, begun, [], 2**34)
     return context_out, query_out.reshape(requests.shape[1:])
 
 

time: 143 us -> 137 us (0.958)
  waiting for transfers between devices: 30.6 us -> 20.7 us
  starting transfers between devices: 66.5 us -> 69.6 us
  Pallas kernels: 31.4 us -> 33.6 us
    all_to_all x2, waiting for transfers between devices: 12.6 us -> 0.53 us  [the longest x1 0.52 us: per_device(): parts = lax.all_to_all(part, 'hst', 0, 0).astype(jnp.float32)]
    pallas_call x2 -> x3, Pallas kernels: 25.1 us -> 28.4 us  [the longest x2 25.2 us: context_part(): pl.pallas_call(kernel, out_shape=jax.ShapeDtypeStruct((rows, cols), jnp.b...]
    ppermute x2, waiting for transfers between devices: 0.01 us -> 2.42 us  [spread_over_group(): return (near, lax.ppermute(near, 'head', [(i, i ^ 1) for i in range(size)]))]
    convert_element_type x1 -> x2, other arithmetic: 0.08 us -> 2 us  [the longest x1 1.14 us: per_device(): parts = lax.all_to_all(part, 'hst', 0, 0).astype(jnp.float32)]
    unnamed x8 -> x14, local copies, waits for them, and re-layouts: 3.36 us -> 3.17 us
  transfers between devices with their start and end apart: 20 -> 20, of which waited for: 5 -> 6; matrix products, arithmetic and copies ran while one was open for 4% -> 3% of each run, Pallas kernels for 22% -> 22%
where the time goes in v3:
time: 137 us; the launch traced here: 136 us
  starting transfers between devices  69.6 us (51%)
  Pallas kernels  33.6 us (25%)
  waiting for transfers between devices  20.7 us (15%)
  local copies, waits for them, and re-layouts  5.11 us (4%)
  other arithmetic  4.87 us (4%)
  between operations  1.67 us (1%)
    pallas_call x2, Pallas kernels, context_part(): pl.pallas_call(kernel, out_shape=jax.ShapeDtypeStruct((rows, cols), jnp.b...  25.2 us
    ppermute x4, starting transfers between devices, send(): return lax.ppermute(x, 'hst', [(a * ny, b * ny) for a, b in pairs])  15.8 us
    ppermute x3, waiting for transfers between devices, spread_anchor(): lax.ppermute(part, 'hst', [(k * ny, k * ny + to) for k in groups])  10.1 us
    all_to_all x1, starting transfers between devices, per_device(): parts = lax.all_to_all(part, 'hst', 0, 0).astype(jnp.float32)  9.66 us
    all_to_all x1, starting transfers between devices, per_device(): query_out = lax.all_to_all(done, 'hst', 0, 0)  8.91 us
    all_to_all x1, starting transfers between devices, per_device(): scattered = lax.all_to_all(pieces, 'hst', 0, 0)  8.72 us
    ppermute x3, starting transfers between devices, spread_anchor(): lax.ppermute(part, 'hst', [(k * ny, k * ny + to) for k in groups])  8.65 us
    ppermute x6, waiting for transfers between devices, spread_over_group(): lax.ppermute(shard, 'head', [(i, (i + step * CORES) % size) for i in rang...  7.61 us
  transfers between devices with their start and end apart: 20, of which 6 were waited for; matrix products, arithmetic and copies ran while one was open for 3% of the time, Pallas kernels for 22%

profile of v3, /device:TPU:1, one launch (start us, length us, event | category | flops | bytes accessed | tf_op | source)
XLA Modules:
  0.0 135.5 jit_solution(3792121311673058870)
XLA Ops:
  2.6 5.5 %collective-permute-start.4 = (bf16[64,2048]{1,0:T(8,128)(2,1)S(1)}, bf16[64,2048]{1,0:T(8,128)(2,1)S(1)}, u32[]{:S(2)}, u32[]{:S(2)}) collective-permute-start(bf16[64,2048]{1,0:T(8,128)(2,1)S(1)} %slice.13), channel_id=1, source_target_pairs={{0,4},{1,5},{2,6},{3,7}} | collective-permute-start | bytes 786440 | tf_op jit(solution)/shard_map/ppermute | solution.py:29
  8.2 2.1 %collective-permute-start.1 = (bf16[128,2048]{1,0:T(8,128)(2,1)S(1)}, bf16[128,2048]{1,0:T(8,128)(2,1)}, u32[]{:S(2)}, u32[]{:S(2)}) collective-permute-start(bf16[128,2048]{1,0:T(8,128)(2,1)S(1)} %constant_dynamic-update-slice_fusion), channel_id=1, source_target_pairs={{0,4},{1,5},{2,6},{3,7},{4,0},{5,1},{6,2},{7,3},{8,12},{9,13},{10,... | collective-permute-start | bytes 1572872 | tf_op jit(solution)/shard_map/ppermute | solution.py:19
  10.3 8.7 %all-to-all-start = ((bf16[32,8,1024]{2,1,0:T(8,128)(2,1)}), bf16[32,8,1024]{2,1,0:T(8,128)(2,1)S(1)}, u32[]{:S(2)}, u32[]{:S(2)}) async-start(bf16[32,8,1024]{2,1,0:T(8,128)(2,1)} %bitcast.19), calls=%async_computation | async-start | bytes 1048576 | tf_op jit(solution)/shard_map/all_to_all | solution.py:216
  19.1 6.9 %collective-permute-start.6 = (bf16[64,2048]{1,0:T(8,128)(2,1)S(1)}, bf16[64,2048]{1,0:T(8,128)(2,1)}, u32[]{:S(2)}, u32[]{:S(2)}) collective-permute-start(bf16[64,2048]{1,0:T(8,128)(2,1)S(1)} %slice_select_fusion), channel_id=1, source_target_pairs={{0,160},{1,161},{2,162},{3,163},{4,164},{5,165},{6,166},{7,167}} | collective-permute-start | bytes 786440 | tf_op jit(solution)/shard_map/ppermute | solution.py:34
  26.0 2.0 %collective-permute-start.5 = (bf16[64,2048]{1,0:T(8,128)(2,1)S(1)}, bf16[64,2048]{1,0:T(8,128)(2,1)}, u32[]{:S(2)}, u32[]{:S(2)}) collective-permute-start(bf16[64,2048]{1,0:T(8,128)(2,1)S(1)} %slice_select_fusion), channel_id=1, source_target_pairs={{0,96},{1,97},{2,98},{3,99},{4,100},{5,101},{6,102},{7,103}} | collective-permute-start | bytes 786440 | tf_op jit(solution)/shard_map/ppermute | solution.py:34
  28.0 7.6 %collective-permute-done = bf16[128,2048]{1,0:T(8,128)(2,1)} collective-permute-done((bf16[128,2048]{1,0:T(8,128)(2,1)S(1)}, bf16[128,2048]{1,0:T(8,128)(2,1)}, u32[]{:S(2)}, u32[]{:S(2)}) %collective-permute-start) | collective-permute-done | bytes 524320 | tf_op jit(solution)/shard_map/ppermute | solution.py:19
  37.1 1.6 %collective-permute-start.3 = (bf16[512,2048]{1,0:T(8,128)(2,1)S(1)}, bf16[512,2048]{1,0:T(8,128)(2,1)}, u32[]{:S(2)}, u32[]{:S(2)}) collective-permute-start(bf16[512,2048]{1,0:T(8,128)(2,1)S(1)} %pad_maximum_fusion.near_key.near_value.refs_0_.refs_4_), channel_id=1, source_target_pairs={{0,1},{1,0},{2,3},{3,2},{4,5},{5,4},{6,7},{7,6},{8,9},{9,8},{10,11... | collective-permute-start | bytes 6291464 | tf_op jit(solution)/shard_map/ppermute | solution.py:23
  38.8 5.0 %collective-permute-start.8 = (bf16[64,2048]{1,0:T(8,128)(2,1)S(1)}, bf16[64,2048]{1,0:T(8,128)(2,1)}, u32[]{:S(2)}, u32[]{:S(2)}) collective-permute-start(bf16[64,2048]{1,0:T(8,128)(2,1)S(1)} %select_select_fusion.2), channel_id=1, source_target_pairs={{0,224},{96,64},{1,225},{97,65},{2,226},{98,66},{3,227},{99,67},{4... | collective-permute-start | bytes 786440 | tf_op jit(solution)/shard_map/ppermute | solution.py:34
  43.7 2.0 %collective-permute-start.7 = (bf16[64,2048]{1,0:T(8,128)(2,1)S(1)}, bf16[64,2048]{1,0:T(8,128)(2,1)}, u32[]{:S(2)}, u32[]{:S(2)}) collective-permute-start(bf16[64,2048]{1,0:T(8,128)(2,1)S(1)} %select_select_fusion.2), channel_id=1, source_target_pairs={{0,32},{96,128},{160,192},{1,33},{97,129},{161,193},{2,34},{98,130... | collective-permute-start | bytes 786440 | tf_op jit(solution)/shard_map/ppermute | solution.py:34
  46.7 4.4 %all-to-all-start.1 = ((bf16[32,8,1024]{2,1,0:T(8,128)(2,1)}), bf16[32,8,1024]{2,1,0:T(8,128)(2,1)S(1)}, u32[]{:S(2)}, u32[]{:S(2)}) async-start(bf16[32,8,1024]{2,1,0:T(8,128)(2,1)} %broadcast_in_dim.9), calls=%async_computation.1 | async-start | bytes 1048576 | tf_op jit(solution)/shard_map/all_to_all | solution.py:218
  51.2 4.7 %collective-permute-start.11 = (bf16[64,2048]{1,0:T(8,128)(2,1)S(1)}, bf16[64,2048]{1,0:T(8,128)(2,1)S(1)}, u32[]{:S(2)}, u32[]{:S(2)}) collective-permute-start(bf16[64,2048]{1,0:T(8,128)(2,1)S(1)} %select_select_fusion.1), channel_id=1, source_target_pairs={{0,16},{32,48},{64,80},{96,112},{128,144},{160,176},{192,208},{224... | collective-permute-start | bytes 786440 | tf_op jit(solution)/shard_map/ppermute | solution.py:42
  55.8 2.0 %collective-permute-start.10 = (bf16[64,2048]{1,0:T(8,128)(2,1)S(1)}, bf16[64,2048]{1,0:T(8,128)(2,1)}, u32[]{:S(2)}, u32[]{:S(2)}) collective-permute-start(bf16[64,2048]{1,0:T(8,128)(2,1)S(1)} %select_select_fusion.1), channel_id=1, source_target_pairs={{0,24},{32,56},{64,88},{96,120},{128,152},{160,184},{192,216},{224... | collective-permute-start | bytes 786440 | tf_op jit(solution)/shard_map/ppermute | solution.py:42
  57.9 2.0 %collective-permute-start.9 = (bf16[64,2048]{1,0:T(8,128)(2,1)S(1)}, bf16[64,2048]{1,0:T(8,128)(2,1)}, u32[]{:S(2)}, u32[]{:S(2)}) collective-permute-start(bf16[64,2048]{1,0:T(8,128)(2,1)S(1)} %select_select_fusion.1), channel_id=1, source_target_pairs={{0,8},{32,40},{64,72},{96,104},{128,136},{160,168},{192,200},{224,... | collective-permute-start | bytes 786440 | tf_op jit(solution)/shard_map/ppermute | solution.py:42
  59.8 3.8 %collective-permute-done.11 = bf16[64,2048]{1,0:T(8,128)(2,1)S(1)} collective-permute-done((bf16[64,2048]{1,0:T(8,128)(2,1)S(1)}, bf16[64,2048]{1,0:T(8,128)(2,1)S(1)}, u32[]{:S(2)}, u32[]{:S(2)}) %collective-permute-start.11) | collective-permute-done | bytes 262176 | tf_op jit(solution)/shard_map/ppermute | solution.py:42
  63.6 1.8 %collective-permute-done.10 = bf16[64,2048]{1,0:T(8,128)(2,1)} collective-permute-done((bf16[64,2048]{1,0:T(8,128)(2,1)S(1)}, bf16[64,2048]{1,0:T(8,128)(2,1)}, u32[]{:S(2)}, u32[]{:S(2)}) %collective-permute-start.10) | collective-permute-done | bytes 262176 | tf_op jit(solution)/shard_map/ppermute | solution.py:42
  65.4 4.6 %collective-permute-done.9 = bf16[64,2048]{1,0:T(8,128)(2,1)} collective-permute-done((bf16[64,2048]{1,0:T(8,128)(2,1)S(1)}, bf16[64,2048]{1,0:T(8,128)(2,1)}, u32[]{:S(2)}, u32[]{:S(2)}) %collective-permute-start.9) | collective-permute-done | bytes 262176 | tf_op jit(solution)/shard_map/ppermute | solution.py:42
  72.3 5.1 %query_part.1 = f32[32,8,1152]{2,1,0:T(8,128)S(1)} custom-call(s32[11]{0:T(128)S(1)} %stack.43.scal, bf16[256,1024]{1,0:T(8,128)(2,1)S(1)} %bitcast.17, bf16[512,2048]{1,0:T(8,128)(2,1)S(1)} %pad_maximum_fusion.near_key.near_value.refs_0_.refs_4_, bf16[512,2048]{1,0:T(8,128)(2,1)} %collective-permute-done.3.far_key.far_value.refs_1_.refs_5_, ...), custom_call_target="tpu_custom_call" | custom-call | flops 2147483648 | bytes 4194304 | tf_op jit(solution)/shard_map/query_part/pallas_call | solution.py:101
  78.4 9.7 %all-to-all-start.2 = ((f16[32,8,1152]{2,1,0:T(8,128)(2,1)}), f16[32,8,1152]{2,1,0:T(8,128)(2,1)}, u32[]{:S(2)}, u32[]{:S(2)}) async-start(f16[32,8,1152]{2,1,0:T(8,128)(2,1)} %convert_element_type.6), calls=%async_computation.2 | async-start | bytes 1179648 | tf_op jit(solution)/shard_map/all_to_all | solution.py:228
  90.6 2.6 %collective-permute-start.15 = (bf16[256,2048]{1,0:T(8,128)(2,1)S(1)}, bf16[256,2048]{1,0:T(8,128)(2,1)}, u32[]{:S(2)}, u32[]{:S(2)}) collective-permute-start(bf16[256,2048]{1,0:T(8,128)(2,1)S(1)} %pad_maximum_fusion.1.refs_2_.refs_6_), channel_id=1, source_target_pairs={{0,1},{1,0},{2,3},{3,2},{4,5},{5,4},{6,7},{7,6},{8,9},{9,8},{10,11... | collective-permute-start | bytes 3145736 | tf_op jit(solution)/shard_map/ppermute | solution.py:23
  93.3 2.4 %collective-permute-done.15.refs_3_.refs_7_ = bf16[256,2048]{1,0:T(8,128)(2,1)} collective-permute-done((bf16[256,2048]{1,0:T(8,128)(2,1)S(1)}, bf16[256,2048]{1,0:T(8,128)(2,1)}, u32[]{:S(2)}, u32[]{:S(2)}) %collective-permute-start.15) | collective-permute-done | bytes 1048608 | tf_op jit(solution)/shard_map/ppermute | solution.py:23
  95.7 7.6 %context_part.2.refs_8_ = bf16[128,8192]{1,0:T(8,128)(2,1)} custom-call(s32[11]{0:T(128)} %copy-done.1, bf16[128,8192]{1,0:T(8,128)(2,1)} %query.3, bf16[512,2048]{1,0:T(8,128)(2,1)} %copy-done, bf16[512,2048]{1,0:T(8,128)(2,1)} %collective-permute-done.3.far_key.far_value.refs_1_.refs_5_, bf16[256,2048]{1,0:T(8,128)(2,1)} %copy-done.2, ...), custom_call_target="tpu_custom_call" | custom-call | flops 1048576 | bytes 1024 | tf_op jit(solution)/shard_map/context_part/pallas_call | solution.py:195
  105.0 3.2 %merge_parts.1 = bf16[32,8,1024]{2,1,0:T(8,128)(2,1)} custom-call(f32[32,8,1152]{2,1,0:T(8,128)S(1)} %convert_element_type.7.parts), custom_call_target="tpu_custom_call" | custom-call | flops 1048576 | bytes 2097152 | tf_op jit(solution)/shard_map/merge_parts/pallas_call | solution.py:139
  108.2 8.9 %all-to-all-start.3 = ((bf16[32,8,1024]{2,1,0:T(8,128)(2,1)}), bf16[32,8,1024]{2,1,0:T(8,128)(2,1)S(1)}, u32[]{:S(2)}, u32[]{:S(2)}) async-start(bf16[32,8,1024]{2,1,0:T(8,128)(2,1)} %merge_parts.1), calls=%async_computation.3 | async-start | bytes 1048576 | tf_op jit(solution)/shard_map/all_to_all | solution.py:233
  117.1 17.6 %context_part.3 = bf16[128,8192]{1,0:T(8,128)(2,1)} custom-call(s32[11]{0:T(128)} %copy-done.1, bf16[128,8192]{1,0:T(8,128)(2,1)} %query.3, bf16[512,2048]{1,0:T(8,128)(2,1)} %copy-done, bf16[512,2048]{1,0:T(8,128)(2,1)} %collective-permute-done.3.far_key.far_value.refs_1_.refs_5_, bf16[256,2048]{1,0:T(8,128)(2,1)} %copy-done.2, ...), custom_call_target="tpu_custom_call", output_to_operand_aliasing={{}: (10, {})} | custom-call | flops 17179869184 | bytes 1024 | tf_op jit(solution)/shard_map/context_part/pallas_call | solution.py:195
  (47 shorter events, 12.2 us)
Async XLA Ops:
  2.6 16.4 %collective-permute-start.4 = (bf16[64,2048]{1,0:T(8,128)(2,1)S(1)}, bf16[64,2048]{1,0:T(8,128)(2,1)S(1)}, u32[]{:S(2)}, u32[]{:S(2)}) collective-permute-start(bf16[64,2048]{1,0:T(8,128)(2,1)S(1)} %slice.13), channel_id=1, source_target_pairs={{0,4},{1,5},{2,6},{3,7}} | collective-permute-start | bytes 786440 | tf_op jit(solution)/shard_map/ppermute | solution.py:29
  8.1 19.8 %collective-permute-start.2 = (bf16[128,2048]{1,0:T(8,128)(2,1)S(1)}, bf16[128,2048]{1,0:T(8,128)(2,1)}, u32[]{:S(2)}, u32[]{:S(2)}) collective-permute-start(bf16[128,2048]{1,0:T(8,128)(2,1)S(1)} %constant_dynamic-update-slice_fusion), channel_id=1, source_target_pairs={{0,6},{1,7},{2,0},{3,1},{4,2},{5,3},{6,4},{7,5},{8,14},{9,15},{10,... | collective-permute-start | bytes 1572872 | tf_op jit(solution)/shard_map/ppermute | solution.py:19
  8.2 19.8 %collective-permute-start.1 = (bf16[128,2048]{1,0:T(8,128)(2,1)S(1)}, bf16[128,2048]{1,0:T(8,128)(2,1)}, u32[]{:S(2)}, u32[]{:S(2)}) collective-permute-start(bf16[128,2048]{1,0:T(8,128)(2,1)S(1)} %constant_dynamic-update-slice_fusion), channel_id=1, source_target_pairs={{0,4},{1,5},{2,6},{3,7},{4,0},{5,1},{6,2},{7,3},{8,12},{9,13},{10,... | collective-permute-start | bytes 1572872 | tf_op jit(solution)/shard_map/ppermute | solution.py:19
  10.3 25.3 %collective-permute-start = (bf16[128,2048]{1,0:T(8,128)(2,1)S(1)}, bf16[128,2048]{1,0:T(8,128)(2,1)}, u32[]{:S(2)}, u32[]{:S(2)}) collective-permute-start(bf16[128,2048]{1,0:T(8,128)(2,1)S(1)} %constant_dynamic-update-slice_fusion), channel_id=1, source_target_pairs={{0,2},{1,3},{2,4},{3,5},{4,6},{5,7},{6,0},{7,1},{8,10},{9,11},{10,... | collective-permute-start | bytes 1572872 | tf_op jit(solution)/shard_map/ppermute | solution.py:19
  10.3 35.6 %all-to-all-start = ((bf16[32,8,1024]{2,1,0:T(8,128)(2,1)}), bf16[32,8,1024]{2,1,0:T(8,128)(2,1)S(1)}, u32[]{:S(2)}, u32[]{:S(2)}) async-start(bf16[32,8,1024]{2,1,0:T(8,128)(2,1)} %bitcast.19), calls=%async_computation | async-start | bytes 1048576 | tf_op jit(solution)/shard_map/all_to_all | solution.py:216
  19.1 26.6 %copy-start.5 = (s32[32]{0:T(128)S(1)}, s32[32]{0:T(128)}, u32[]{:S(2)}) copy-start(s32[32]{0:T(128)} %param.11) | copy-start | bytes 388
  19.1 19.6 %collective-permute-start.6 = (bf16[64,2048]{1,0:T(8,128)(2,1)S(1)}, bf16[64,2048]{1,0:T(8,128)(2,1)}, u32[]{:S(2)}, u32[]{:S(2)}) collective-permute-start(bf16[64,2048]{1,0:T(8,128)(2,1)S(1)} %slice_select_fusion), channel_id=1, source_target_pairs={{0,160},{1,161},{2,162},{3,163},{4,164},{5,165},{6,166},{7,167}} | collective-permute-start | bytes 786440 | tf_op jit(solution)/shard_map/ppermute | solution.py:34
  26.0 12.8 %collective-permute-start.5 = (bf16[64,2048]{1,0:T(8,128)(2,1)S(1)}, bf16[64,2048]{1,0:T(8,128)(2,1)}, u32[]{:S(2)}, u32[]{:S(2)}) collective-permute-start(bf16[64,2048]{1,0:T(8,128)(2,1)S(1)} %slice_select_fusion), channel_id=1, source_target_pairs={{0,96},{1,97},{2,98},{3,99},{4,100},{5,101},{6,102},{7,103}} | collective-permute-start | bytes 786440 | tf_op jit(solution)/shard_map/ppermute | solution.py:34
  37.1 35.3 %copy-start = (bf16[512,2048]{1,0:T(8,128)(2,1)}, bf16[512,2048]{1,0:T(8,128)(2,1)S(1)}, u32[]{:S(2)}) copy-start(bf16[512,2048]{1,0:T(8,128)(2,1)S(1)} %pad_maximum_fusion.near_key.near_value.refs_0_.refs_4_) | copy-start | bytes 6291460
  37.1 35.2 %collective-permute-start.3 = (bf16[512,2048]{1,0:T(8,128)(2,1)S(1)}, bf16[512,2048]{1,0:T(8,128)(2,1)}, u32[]{:S(2)}, u32[]{:S(2)}) collective-permute-start(bf16[512,2048]{1,0:T(8,128)(2,1)S(1)} %pad_maximum_fusion.near_key.near_value.refs_0_.refs_4_), channel_id=1, source_target_pairs={{0,1},{1,0},{2,3},{3,2},{4,5},{5,4},{6,7},{7,6},{8,9},{9,8},{10,11... | collective-permute-start | bytes 6291464 | tf_op jit(solution)/shard_map/ppermute | solution.py:23
  38.8 12.3 %collective-permute-start.8 = (bf16[64,2048]{1,0:T(8,128)(2,1)S(1)}, bf16[64,2048]{1,0:T(8,128)(2,1)}, u32[]{:S(2)}, u32[]{:S(2)}) collective-permute-start(bf16[64,2048]{1,0:T(8,128)(2,1)S(1)} %select_select_fusion.2), channel_id=1, source_target_pairs={{0,224},{96,64},{1,225},{97,65},{2,226},{98,66},{3,227},{99,67},{4... | collective-permute-start | bytes 786440 | tf_op jit(solution)/shard_map/ppermute | solution.py:34
  43.7 7.4 %collective-permute-start.7 = (bf16[64,2048]{1,0:T(8,128)(2,1)S(1)}, bf16[64,2048]{1,0:T(8,128)(2,1)}, u32[]{:S(2)}, u32[]{:S(2)}) collective-permute-start(bf16[64,2048]{1,0:T(8,128)(2,1)S(1)} %select_select_fusion.2), channel_id=1, source_target_pairs={{0,32},{96,128},{160,192},{1,33},{97,129},{161,193},{2,34},{98,130... | collective-permute-start | bytes 786440 | tf_op jit(solution)/shard_map/ppermute | solution.py:34
  46.7 25.6 %all-to-all-start.1 = ((bf16[32,8,1024]{2,1,0:T(8,128)(2,1)}), bf16[32,8,1024]{2,1,0:T(8,128)(2,1)S(1)}, u32[]{:S(2)}, u32[]{:S(2)}) async-start(bf16[32,8,1024]{2,1,0:T(8,128)(2,1)} %broadcast_in_dim.9), calls=%async_computation.1 | async-start | bytes 1048576 | tf_op jit(solution)/shard_map/all_to_all | solution.py:218
  51.2 12.4 %collective-permute-start.11 = (bf16[64,2048]{1,0:T(8,128)(2,1)S(1)}, bf16[64,2048]{1,0:T(8,128)(2,1)S(1)}, u32[]{:S(2)}, u32[]{:S(2)}) collective-permute-start(bf16[64,2048]{1,0:T(8,128)(2,1)S(1)} %select_select_fusion.1), channel_id=1, source_target_pairs={{0,16},{32,48},{64,80},{96,112},{128,144},{160,176},{192,208},{224... | collective-permute-start | bytes 786440 | tf_op jit(solution)/shard_map/ppermute | solution.py:42
  55.8 9.5 %collective-permute-start.10 = (bf16[64,2048]{1,0:T(8,128)(2,1)S(1)}, bf16[64,2048]{1,0:T(8,128)(2,1)}, u32[]{:S(2)}, u32[]{:S(2)}) collective-permute-start(bf16[64,2048]{1,0:T(8,128)(2,1)S(1)} %select_select_fusion.1), channel_id=1, source_target_pairs={{0,24},{32,56},{64,88},{96,120},{128,152},{160,184},{192,216},{224... | collective-permute-start | bytes 786440 | tf_op jit(solution)/shard_map/ppermute | solution.py:42
  57.9 12.1 %collective-permute-start.9 = (bf16[64,2048]{1,0:T(8,128)(2,1)S(1)}, bf16[64,2048]{1,0:T(8,128)(2,1)}, u32[]{:S(2)}, u32[]{:S(2)}) collective-permute-start(bf16[64,2048]{1,0:T(8,128)(2,1)S(1)} %select_select_fusion.1), channel_id=1, source_target_pairs={{0,8},{32,40},{64,72},{96,104},{128,136},{160,168},{192,200},{224,... | collective-permute-start | bytes 786440 | tf_op jit(solution)/shard_map/ppermute | solution.py:42
  70.0 18.0 %collective-permute-start.14 = (bf16[64,2048]{1,0:T(8,128)(2,1)S(1)}, bf16[64,2048]{1,0:T(8,128)(2,1)S(1)}, u32[]{:S(2)}, u32[]{:S(2)}) collective-permute-start(bf16[64,2048]{1,0:T(8,128)(2,1)S(1)} %select_select_fusion.after), channel_id=1, source_target_pairs={{0,6},{1,7},{2,0},{3,1},{4,2},{5,3},{6,4},{7,5},{8,14},{9,15},{10,... | collective-permute-start | bytes 786440 | tf_op jit(solution)/shard_map/ppermute | solution.py:19
  70.3 17.8 %collective-permute-start.13 = (bf16[64,2048]{1,0:T(8,128)(2,1)S(1)}, bf16[64,2048]{1,0:T(8,128)(2,1)S(1)}, u32[]{:S(2)}, u32[]{:S(2)}) collective-permute-start(bf16[64,2048]{1,0:T(8,128)(2,1)S(1)} %select_select_fusion.after), channel_id=1, source_target_pairs={{0,4},{1,5},{2,6},{3,7},{4,0},{5,1},{6,2},{7,3},{8,12},{9,13},{10,... | collective-permute-start | bytes 786440 | tf_op jit(solution)/shard_map/ppermute | solution.py:19
  70.7 18.7 %collective-permute-start.12 = (bf16[64,2048]{1,0:T(8,128)(2,1)S(1)}, bf16[64,2048]{1,0:T(8,128)(2,1)}, u32[]{:S(2)}, u32[]{:S(2)}) collective-permute-start(bf16[64,2048]{1,0:T(8,128)(2,1)S(1)} %select_select_fusion.after), channel_id=1, source_target_pairs={{0,2},{1,3},{2,4},{3,5},{4,6},{5,7},{6,0},{7,1},{8,10},{9,11},{10,... | collective-permute-start | bytes 786440 | tf_op jit(solution)/shard_map/ppermute | solution.py:19
  72.3 5.2 %copy-start.1 = (s32[11]{0:T(128)}, s32[11]{0:T(128)S(1)}, u32[]{:S(2)}) copy-start(s32[11]{0:T(128)S(1)} %stack.43.scal) | copy-start | bytes 136
  78.4 25.5 %all-to-all-start.2 = ((f16[32,8,1152]{2,1,0:T(8,128)(2,1)}), f16[32,8,1152]{2,1,0:T(8,128)(2,1)}, u32[]{:S(2)}, u32[]{:S(2)}) async-start(f16[32,8,1152]{2,1,0:T(8,128)(2,1)} %convert_element_type.6), calls=%async_computation.2 | async-start | bytes 1179648 | tf_op jit(solution)/shard_map/all_to_all | solution.py:228
  90.6 5.1 %copy-start.2 = (bf16[256,2048]{1,0:T(8,128)(2,1)}, bf16[256,2048]{1,0:T(8,128)(2,1)S(1)}, u32[]{:S(2)}) copy-start(bf16[256,2048]{1,0:T(8,128)(2,1)S(1)} %pad_maximum_fusion.1.refs_2_.refs_6_) | copy-start | bytes 3145732
  90.6 5.1 %collective-permute-start.15 = (bf16[256,2048]{1,0:T(8,128)(2,1)S(1)}, bf16[256,2048]{1,0:T(8,128)(2,1)}, u32[]{:S(2)}, u32[]{:S(2)}) collective-permute-start(bf16[256,2048]{1,0:T(8,128)(2,1)S(1)} %pad_maximum_fusion.1.refs_2_.refs_6_), channel_id=1, source_target_pairs={{0,1},{1,0},{2,3},{3,2},{4,5},{5,4},{6,7},{7,6},{8,9},{9,8},{10,11... | collective-permute-start | bytes 3145736 | tf_op jit(solution)/shard_map/ppermute | solution.py:23
  108.2 26.5 %all-to-all-start.3 = ((bf16[32,8,1024]{2,1,0:T(8,128)(2,1)}), bf16[32,8,1024]{2,1,0:T(8,128)(2,1)S(1)}, u32[]{:S(2)}, u32[]{:S(2)}) async-start(bf16[32,8,1024]{2,1,0:T(8,128)(2,1)} %merge_parts.1), calls=%async_computation.3 | async-start | bytes 1048576 | tf_op jit(solution)/shard_map/all_to_all | solution.py:233
  (2 other events, 1.4 us)

commit v4 on v3

--- a/solution.py
+++ b/solution.py
@@ -117,21 +117,22 @@
 
 def merge_kernel(parts, out):
     heads = out.shape[2] // DH
-
-    def stat(at, a):
-        lane = heads * DH + at * heads + a
-        return parts[:, :, lane : lane + 1]
-
+    stats = parts[:, :, heads * DH :]
+
+    def lane(x, at):
+        return pltpu.roll(x, (DH - at * heads) % DH, 2)
+
+    whole = stats + lane(stats, 1) + lane(stats, 2)
+    top, total = whole, lane(whole, 3)
+    front = lax.broadcasted_iota(jnp.int32, stats.shape, 2) < heads
+    scale = jnp.where(front, jnp.exp2(top - jnp.max(top, axis=0, keepdims=True)), 0.0)
+    total_all = jnp.sum(total * scale, axis=0, keepdims=True)
+    power = jnp.where(front, lane(stats, 6), 0.0)
+    factor = scale * jnp.exp2(power) / jnp.where(front[:1], total_all, 1.0)
     for a in range(heads):
-        top = stat(0, a) + stat(1, a) + stat(2, a)
-        total = stat(3, a) + stat(4, a) + stat(5, a)
-        best = jnp.max(top, axis=0, keepdims=True)
-        scale = jnp.exp2(top - best)
-        total_all = jnp.sum(total * scale, axis=0)
-        scale = scale * jnp.exp2(stat(6, a))
-        summed = jnp.sum(parts[:, :, a * DH : (a + 1) * DH] * scale, axis=0)
-        done = (summed / total_all).astype(out.dtype)
-        out[:, :, a * DH : (a + 1) * DH] = jnp.broadcast_to(done[None], (out.shape[0],) + done.shape)
+        column = slice(a * DH, (a + 1) * DH)
+        done = jnp.sum(parts[:, :, column] * factor[:, :, a : a + 1], axis=0).astype(out.dtype)
+        out[:, :, column] = jnp.broadcast_to(done[None], (out.shape[0],) + done.shape)
 
 
 def merge_parts(parts):

time: 137 us -> 135 us (0.985)
  Pallas kernels: 33.6 us -> 31.8 us
    pallas_call x1, Pallas kernels: 3.23 us -> 1.42 us  [merge_parts(): pl.pallas_call(merge_kernel, out_shape=jax.ShapeDtypeStruct((n, rows, col...]
  transfers between devices with their start and end apart: 20 -> 20, of which waited for: 6 -> 6; matrix products, arithmetic and copies ran while one was open for 3% -> 3% of each run, Pallas kernels for 22% -> 23%
where the time goes in v4:
time: 135 us; the launch traced here: 134 us
  starting transfers between devices  69.6 us (52%)
  Pallas kernels  31.8 us (24%)
  waiting for transfers between devices  20.7 us (15%)
  local copies, waits for them, and re-layouts  5.11 us (4%)
  other arithmetic  4.87 us (4%)
  between operations  1.67 us (1%)
    pallas_call x2, Pallas kernels, context_part(): pl.pallas_call(kernel, out_shape=jax.ShapeDtypeStruct((rows, cols), jnp.b...  25.2 us
    ppermute x4, starting transfers between devices, send(): return lax.ppermute(x, 'hst', [(a * ny, b * ny) for a, b in pairs])  15.8 us
    ppermute x3, waiting for transfers between devices, spread_anchor(): lax.ppermute(part, 'hst', [(k * ny, k * ny + to) for k in groups])  10.1 us
    all_to_all x1, starting transfers between devices, per_device(): parts = lax.all_to_all(part, 'hst', 0, 0).astype(jnp.float32)  9.66 us
    all_to_all x1, starting transfers between devices, per_device(): query_out = lax.all_to_all(done, 'hst', 0, 0)  8.91 us
    all_to_all x1, starting transfers between devices, per_device(): scattered = lax.all_to_all(pieces, 'hst', 0, 0)  8.72 us
    ppermute x3, starting transfers between devices, spread_anchor(): lax.ppermute(part, 'hst', [(k * ny, k * ny + to) for k in groups])  8.65 us
    ppermute x6, waiting for transfers between devices, spread_over_group(): lax.ppermute(shard, 'head', [(i, (i + step * CORES) % size) for i in rang...  7.61 us
  transfers between devices with their start and end apart: 20, of which 6 were waited for; matrix products, arithmetic and copies ran while one was open for 3% of the time, Pallas kernels for 23%

profile of v4, /device:TPU:1, one launch (start us, length us, event | category | flops | bytes accessed | tf_op | source)
XLA Modules:
  0.0 133.7 jit_solution(9567867673991630922)
XLA Ops:
  2.6 5.5 %collective-permute-start.4 = (bf16[64,2048]{1,0:T(8,128)(2,1)S(1)}, bf16[64,2048]{1,0:T(8,128)(2,1)S(1)}, u32[]{:S(2)}, u32[]{:S(2)}) collective-permute-start(bf16[64,2048]{1,0:T(8,128)(2,1)S(1)} %slice.13), channel_id=1, source_target_pairs={{0,4},{1,5},{2,6},{3,7}} | collective-permute-start | bytes 786440 | tf_op jit(solution)/shard_map/ppermute | solution.py:29
  8.2 2.1 %collective-permute-start.1 = (bf16[128,2048]{1,0:T(8,128)(2,1)S(1)}, bf16[128,2048]{1,0:T(8,128)(2,1)}, u32[]{:S(2)}, u32[]{:S(2)}) collective-permute-start(bf16[128,2048]{1,0:T(8,128)(2,1)S(1)} %constant_dynamic-update-slice_fusion), channel_id=1, source_target_pairs={{0,4},{1,5},{2,6},{3,7},{4,0},{5,1},{6,2},{7,3},{8,12},{9,13},{10,... | collective-permute-start | bytes 1572872 | tf_op jit(solution)/shard_map/ppermute | solution.py:19
  10.3 8.7 %all-to-all-start = ((bf16[32,8,1024]{2,1,0:T(8,128)(2,1)}), bf16[32,8,1024]{2,1,0:T(8,128)(2,1)S(1)}, u32[]{:S(2)}, u32[]{:S(2)}) async-start(bf16[32,8,1024]{2,1,0:T(8,128)(2,1)} %bitcast.19), calls=%async_computation | async-start | bytes 1048576 | tf_op jit(solution)/shard_map/all_to_all | solution.py:217
  19.1 6.9 %collective-permute-start.6 = (bf16[64,2048]{1,0:T(8,128)(2,1)S(1)}, bf16[64,2048]{1,0:T(8,128)(2,1)}, u32[]{:S(2)}, u32[]{:S(2)}) collective-permute-start(bf16[64,2048]{1,0:T(8,128)(2,1)S(1)} %slice_select_fusion), channel_id=1, source_target_pairs={{0,160},{1,161},{2,162},{3,163},{4,164},{5,165},{6,166},{7,167}} | collective-permute-start | bytes 786440 | tf_op jit(solution)/shard_map/ppermute | solution.py:34
  26.0 2.0 %collective-permute-start.5 = (bf16[64,2048]{1,0:T(8,128)(2,1)S(1)}, bf16[64,2048]{1,0:T(8,128)(2,1)}, u32[]{:S(2)}, u32[]{:S(2)}) collective-permute-start(bf16[64,2048]{1,0:T(8,128)(2,1)S(1)} %slice_select_fusion), channel_id=1, source_target_pairs={{0,96},{1,97},{2,98},{3,99},{4,100},{5,101},{6,102},{7,103}} | collective-permute-start | bytes 786440 | tf_op jit(solution)/shard_map/ppermute | solution.py:34
  28.0 7.6 %collective-permute-done = bf16[128,2048]{1,0:T(8,128)(2,1)} collective-permute-done((bf16[128,2048]{1,0:T(8,128)(2,1)S(1)}, bf16[128,2048]{1,0:T(8,128)(2,1)}, u32[]{:S(2)}, u32[]{:S(2)}) %collective-permute-start) | collective-permute-done | bytes 524320 | tf_op jit(solution)/shard_map/ppermute | solution.py:19
  35.6 1.5 %pad_maximum_fusion.near_key.near_value.refs_0_.refs_4_ = bf16[512,2048]{1,0:T(8,128)(2,1)S(1)} fusion(bf16[128,2048]{1,0:T(8,128)(2,1)} %collective-permute-done.2, bf16[128,2048]{1,0:T(8,128)(2,1)} %collective-permute-done.1, bf16[128,2048]{1,0:T(8,128)(2,1)} %collective-permute-done, bf16[128,2048]{1,0:T(8,128)(2,1)S(1)} %constant_dynamic-update-slice_fusion), kind=kLoop, calls=%fused_computation | loop fusion | flops 8388608 | bytes 4194304 | tf_op jit(solution)/shard_map/concatenate | solution.py:22
  37.1 1.6 %collective-permute-start.3 = (bf16[512,2048]{1,0:T(8,128)(2,1)S(1)}, bf16[512,2048]{1,0:T(8,128)(2,1)}, u32[]{:S(2)}, u32[]{:S(2)}) collective-permute-start(bf16[512,2048]{1,0:T(8,128)(2,1)S(1)} %pad_maximum_fusion.near_key.near_value.refs_0_.refs_4_), channel_id=1, source_target_pairs={{0,1},{1,0},{2,3},{3,2},{4,5},{5,4},{6,7},{7,6},{8,9},{9,8},{10,11... | collective-permute-start | bytes 6291464 | tf_op jit(solution)/shard_map/ppermute | solution.py:23
  38.8 5.0 %collective-permute-start.8 = (bf16[64,2048]{1,0:T(8,128)(2,1)S(1)}, bf16[64,2048]{1,0:T(8,128)(2,1)}, u32[]{:S(2)}, u32[]{:S(2)}) collective-permute-start(bf16[64,2048]{1,0:T(8,128)(2,1)S(1)} %select_select_fusion.2), channel_id=1, source_target_pairs={{0,224},{96,64},{1,225},{97,65},{2,226},{98,66},{3,227},{99,67},{4... | collective-permute-start | bytes 786440 | tf_op jit(solution)/shard_map/ppermute | solution.py:34
  43.7 2.0 %collective-permute-start.7 = (bf16[64,2048]{1,0:T(8,128)(2,1)S(1)}, bf16[64,2048]{1,0:T(8,128)(2,1)}, u32[]{:S(2)}, u32[]{:S(2)}) collective-permute-start(bf16[64,2048]{1,0:T(8,128)(2,1)S(1)} %select_select_fusion.2), channel_id=1, source_target_pairs={{0,32},{96,128},{160,192},{1,33},{97,129},{161,193},{2,34},{98,130... | collective-permute-start | bytes 786440 | tf_op jit(solution)/shard_map/ppermute | solution.py:34
  46.7 4.4 %all-to-all-start.1 = ((bf16[32,8,1024]{2,1,0:T(8,128)(2,1)}), bf16[32,8,1024]{2,1,0:T(8,128)(2,1)S(1)}, u32[]{:S(2)}, u32[]{:S(2)}) async-start(bf16[32,8,1024]{2,1,0:T(8,128)(2,1)} %broadcast_in_dim.9), calls=%async_computation.1 | async-start | bytes 1048576 | tf_op jit(solution)/shard_map/all_to_all | solution.py:219
  51.2 4.7 %collective-permute-start.11 = (bf16[64,2048]{1,0:T(8,128)(2,1)S(1)}, bf16[64,2048]{1,0:T(8,128)(2,1)S(1)}, u32[]{:S(2)}, u32[]{:S(2)}) collective-permute-start(bf16[64,2048]{1,0:T(8,128)(2,1)S(1)} %select_select_fusion.1), channel_id=1, source_target_pairs={{0,16},{32,48},{64,80},{96,112},{128,144},{160,176},{192,208},{224... | collective-permute-start | bytes 786440 | tf_op jit(solution)/shard_map/ppermute | solution.py:42
  55.8 2.0 %collective-permute-start.10 = (bf16[64,2048]{1,0:T(8,128)(2,1)S(1)}, bf16[64,2048]{1,0:T(8,128)(2,1)}, u32[]{:S(2)}, u32[]{:S(2)}) collective-permute-start(bf16[64,2048]{1,0:T(8,128)(2,1)S(1)} %select_select_fusion.1), channel_id=1, source_target_pairs={{0,24},{32,56},{64,88},{96,120},{128,152},{160,184},{192,216},{224... | collective-permute-start | bytes 786440 | tf_op jit(solution)/shard_map/ppermute | solution.py:42
  57.9 2.0 %collective-permute-start.9 = (bf16[64,2048]{1,0:T(8,128)(2,1)S(1)}, bf16[64,2048]{1,0:T(8,128)(2,1)}, u32[]{:S(2)}, u32[]{:S(2)}) collective-permute-start(bf16[64,2048]{1,0:T(8,128)(2,1)S(1)} %select_select_fusion.1), channel_id=1, source_target_pairs={{0,8},{32,40},{64,72},{96,104},{128,136},{160,168},{192,200},{224,... | collective-permute-start | bytes 786440 | tf_op jit(solution)/shard_map/ppermute | solution.py:42
  59.8 3.8 %collective-permute-done.11 = bf16[64,2048]{1,0:T(8,128)(2,1)S(1)} collective-permute-done((bf16[64,2048]{1,0:T(8,128)(2,1)S(1)}, bf16[64,2048]{1,0:T(8,128)(2,1)S(1)}, u32[]{:S(2)}, u32[]{:S(2)}) %collective-permute-start.11) | collective-permute-done | bytes 262176 | tf_op jit(solution)/shard_map/ppermute | solution.py:42
  63.6 1.8 %collective-permute-done.10 = bf16[64,2048]{1,0:T(8,128)(2,1)} collective-permute-done((bf16[64,2048]{1,0:T(8,128)(2,1)S(1)}, bf16[64,2048]{1,0:T(8,128)(2,1)}, u32[]{:S(2)}, u32[]{:S(2)}) %collective-permute-start.10) | collective-permute-done | bytes 262176 | tf_op jit(solution)/shard_map/ppermute | solution.py:42
  65.4 4.6 %collective-permute-done.9 = bf16[64,2048]{1,0:T(8,128)(2,1)} collective-permute-done((bf16[64,2048]{1,0:T(8,128)(2,1)S(1)}, bf16[64,2048]{1,0:T(8,128)(2,1)}, u32[]{:S(2)}, u32[]{:S(2)}) %collective-permute-start.9) | collective-permute-done | bytes 262176 | tf_op jit(solution)/shard_map/ppermute | solution.py:42
  72.3 5.1 %query_part.1 = f32[32,8,1152]{2,1,0:T(8,128)S(1)} custom-call(s32[11]{0:T(128)S(1)} %stack.43.scal, bf16[256,1024]{1,0:T(8,128)(2,1)S(1)} %bitcast.17, bf16[512,2048]{1,0:T(8,128)(2,1)S(1)} %pad_maximum_fusion.near_key.near_value.refs_0_.refs_4_, bf16[512,2048]{1,0:T(8,128)(2,1)} %collective-permute-done.3.far_key.far_value.refs_1_.refs_5_, ...), custom_call_target="tpu_custom_call" | custom-call | flops 2147483648 | bytes 4194304 | tf_op jit(solution)/shard_map/query_part/pallas_call | solution.py:101
  78.4 9.7 %all-to-all-start.2 = ((f16[32,8,1152]{2,1,0:T(8,128)(2,1)}), f16[32,8,1152]{2,1,0:T(8,128)(2,1)}, u32[]{:S(2)}, u32[]{:S(2)}) async-start(f16[32,8,1152]{2,1,0:T(8,128)(2,1)} %convert_element_type.6), calls=%async_computation.2 | async-start | bytes 1179648 | tf_op jit(solution)/shard_map/all_to_all | solution.py:229
  90.6 2.6 %collective-permute-start.15 = (bf16[256,2048]{1,0:T(8,128)(2,1)S(1)}, bf16[256,2048]{1,0:T(8,128)(2,1)}, u32[]{:S(2)}, u32[]{:S(2)}) collective-permute-start(bf16[256,2048]{1,0:T(8,128)(2,1)S(1)} %pad_maximum_fusion.1.refs_2_.refs_6_), channel_id=1, source_target_pairs={{0,1},{1,0},{2,3},{3,2},{4,5},{5,4},{6,7},{7,6},{8,9},{9,8},{10,11... | collective-permute-start | bytes 3145736 | tf_op jit(solution)/shard_map/ppermute | solution.py:23
  93.3 2.4 %collective-permute-done.15.refs_3_.refs_7_ = bf16[256,2048]{1,0:T(8,128)(2,1)} collective-permute-done((bf16[256,2048]{1,0:T(8,128)(2,1)S(1)}, bf16[256,2048]{1,0:T(8,128)(2,1)}, u32[]{:S(2)}, u32[]{:S(2)}) %collective-permute-start.15) | collective-permute-done | bytes 1048608 | tf_op jit(solution)/shard_map/ppermute | solution.py:23
  95.7 7.6 %context_part.2.refs_8_ = bf16[128,8192]{1,0:T(8,128)(2,1)} custom-call(s32[11]{0:T(128)} %copy-done.1, bf16[128,8192]{1,0:T(8,128)(2,1)} %query.3, bf16[512,2048]{1,0:T(8,128)(2,1)} %copy-done, bf16[512,2048]{1,0:T(8,128)(2,1)} %collective-permute-done.3.far_key.far_value.refs_1_.refs_5_, bf16[256,2048]{1,0:T(8,128)(2,1)} %copy-done.2, ...), custom_call_target="tpu_custom_call" | custom-call | flops 1048576 | bytes 1024 | tf_op jit(solution)/shard_map/context_part/pallas_call | solution.py:196
  106.4 8.9 %all-to-all-start.3 = ((bf16[32,8,1024]{2,1,0:T(8,128)(2,1)}), bf16[32,8,1024]{2,1,0:T(8,128)(2,1)S(1)}, u32[]{:S(2)}, u32[]{:S(2)}) async-start(bf16[32,8,1024]{2,1,0:T(8,128)(2,1)} %merge_parts.1), calls=%async_computation.3 | async-start | bytes 1048576 | tf_op jit(solution)/shard_map/all_to_all | solution.py:234
  115.3 17.6 %context_part.3 = bf16[128,8192]{1,0:T(8,128)(2,1)} custom-call(s32[11]{0:T(128)} %copy-done.1, bf16[128,8192]{1,0:T(8,128)(2,1)} %query.3, bf16[512,2048]{1,0:T(8,128)(2,1)} %copy-done, bf16[512,2048]{1,0:T(8,128)(2,1)} %collective-permute-done.3.far_key.far_value.refs_1_.refs_5_, bf16[256,2048]{1,0:T(8,128)(2,1)} %copy-done.2, ...), custom_call_target="tpu_custom_call", output_to_operand_aliasing={{}: (10, {})} | custom-call | flops 17179869184 | bytes 1024 | tf_op jit(solution)/shard_map/context_part/pallas_call | solution.py:196
  (47 shorter events, 12.1 us)
Async XLA Ops:
  2.6 16.4 %collective-permute-start.4 = (bf16[64,2048]{1,0:T(8,128)(2,1)S(1)}, bf16[64,2048]{1,0:T(8,128)(2,1)S(1)}, u32[]{:S(2)}, u32[]{:S(2)}) collective-permute-start(bf16[64,2048]{1,0:T(8,128)(2,1)S(1)} %slice.13), channel_id=1, source_target_pairs={{0,4},{1,5},{2,6},{3,7}} | collective-permute-start | bytes 786440 | tf_op jit(solution)/shard_map/ppermute | solution.py:29
  8.1 19.8 %collective-permute-start.2 = (bf16[128,2048]{1,0:T(8,128)(2,1)S(1)}, bf16[128,2048]{1,0:T(8,128)(2,1)}, u32[]{:S(2)}, u32[]{:S(2)}) collective-permute-start(bf16[128,2048]{1,0:T(8,128)(2,1)S(1)} %constant_dynamic-update-slice_fusion), channel_id=1, source_target_pairs={{0,6},{1,7},{2,0},{3,1},{4,2},{5,3},{6,4},{7,5},{8,14},{9,15},{10,... | collective-permute-start | bytes 1572872 | tf_op jit(solution)/shard_map/ppermute | solution.py:19
  8.2 19.8 %collective-permute-start.1 = (bf16[128,2048]{1,0:T(8,128)(2,1)S(1)}, bf16[128,2048]{1,0:T(8,128)(2,1)}, u32[]{:S(2)}, u32[]{:S(2)}) collective-permute-start(bf16[128,2048]{1,0:T(8,128)(2,1)S(1)} %constant_dynamic-update-slice_fusion), channel_id=1, source_target_pairs={{0,4},{1,5},{2,6},{3,7},{4,0},{5,1},{6,2},{7,3},{8,12},{9,13},{10,... | collective-permute-start | bytes 1572872 | tf_op jit(solution)/shard_map/ppermute | solution.py:19
  10.3 25.3 %collective-permute-start = (bf16[128,2048]{1,0:T(8,128)(2,1)S(1)}, bf16[128,2048]{1,0:T(8,128)(2,1)}, u32[]{:S(2)}, u32[]{:S(2)}) collective-permute-start(bf16[128,2048]{1,0:T(8,128)(2,1)S(1)} %constant_dynamic-update-slice_fusion), channel_id=1, source_target_pairs={{0,2},{1,3},{2,4},{3,5},{4,6},{5,7},{6,0},{7,1},{8,10},{9,11},{10,... | collective-permute-start | bytes 1572872 | tf_op jit(solution)/shard_map/ppermute | solution.py:19
  10.3 35.6 %all-to-all-start = ((bf16[32,8,1024]{2,1,0:T(8,128)(2,1)}), bf16[32,8,1024]{2,1,0:T(8,128)(2,1)S(1)}, u32[]{:S(2)}, u32[]{:S(2)}) async-start(bf16[32,8,1024]{2,1,0:T(8,128)(2,1)} %bitcast.19), calls=%async_computation | async-start | bytes 1048576 | tf_op jit(solution)/shard_map/all_to_all | solution.py:217
  19.1 26.6 %copy-start.5 = (s32[32]{0:T(128)S(1)}, s32[32]{0:T(128)}, u32[]{:S(2)}) copy-start(s32[32]{0:T(128)} %param.11) | copy-start | bytes 388
  19.1 19.6 %collective-permute-start.6 = (bf16[64,2048]{1,0:T(8,128)(2,1)S(1)}, bf16[64,2048]{1,0:T(8,128)(2,1)}, u32[]{:S(2)}, u32[]{:S(2)}) collective-permute-start(bf16[64,2048]{1,0:T(8,128)(2,1)S(1)} %slice_select_fusion), channel_id=1, source_target_pairs={{0,160},{1,161},{2,162},{3,163},{4,164},{5,165},{6,166},{7,167}} | collective-permute-start | bytes 786440 | tf_op jit(solution)/shard_map/ppermute | solution.py:34
  26.0 12.8 %collective-permute-start.5 = (bf16[64,2048]{1,0:T(8,128)(2,1)S(1)}, bf16[64,2048]{1,0:T(8,128)(2,1)}, u32[]{:S(2)}, u32[]{:S(2)}) collective-permute-start(bf16[64,2048]{1,0:T(8,128)(2,1)S(1)} %slice_select_fusion), channel_id=1, source_target_pairs={{0,96},{1,97},{2,98},{3,99},{4,100},{5,101},{6,102},{7,103}} | collective-permute-start | bytes 786440 | tf_op jit(solution)/shard_map/ppermute | solution.py:34
  37.1 35.3 %copy-start = (bf16[512,2048]{1,0:T(8,128)(2,1)}, bf16[512,2048]{1,0:T(8,128)(2,1)S(1)}, u32[]{:S(2)}) copy-start(bf16[512,2048]{1,0:T(8,128)(2,1)S(1)} %pad_maximum_fusion.near_key.near_value.refs_0_.refs_4_) | copy-start | bytes 6291460
  37.1 35.2 %collective-permute-start.3 = (bf16[512,2048]{1,0:T(8,128)(2,1)S(1)}, bf16[512,2048]{1,0:T(8,128)(2,1)}, u32[]{:S(2)}, u32[]{:S(2)}) collective-permute-start(bf16[512,2048]{1,0:T(8,128)(2,1)S(1)} %pad_maximum_fusion.near_key.near_value.refs_0_.refs_4_), channel_id=1, source_target_pairs={{0,1},{1,0},{2,3},{3,2},{4,5},{5,4},{6,7},{7,6},{8,9},{9,8},{10,11... | collective-permute-start | bytes 6291464 | tf_op jit(solution)/shard_map/ppermute | solution.py:23
  38.8 12.3 %collective-permute-start.8 = (bf16[64,2048]{1,0:T(8,128)(2,1)S(1)}, bf16[64,2048]{1,0:T(8,128)(2,1)}, u32[]{:S(2)}, u32[]{:S(2)}) collective-permute-start(bf16[64,2048]{1,0:T(8,128)(2,1)S(1)} %select_select_fusion.2), channel_id=1, source_target_pairs={{0,224},{96,64},{1,225},{97,65},{2,226},{98,66},{3,227},{99,67},{4... | collective-permute-start | bytes 786440 | tf_op jit(solution)/shard_map/ppermute | solution.py:34
  43.7 7.4 %collective-permute-start.7 = (bf16[64,2048]{1,0:T(8,128)(2,1)S(1)}, bf16[64,2048]{1,0:T(8,128)(2,1)}, u32[]{:S(2)}, u32[]{:S(2)}) collective-permute-start(bf16[64,2048]{1,0:T(8,128)(2,1)S(1)} %select_select_fusion.2), channel_id=1, source_target_pairs={{0,32},{96,128},{160,192},{1,33},{97,129},{161,193},{2,34},{98,130... | collective-permute-start | bytes 786440 | tf_op jit(solution)/shard_map/ppermute | solution.py:34
  46.7 25.6 %all-to-all-start.1 = ((bf16[32,8,1024]{2,1,0:T(8,128)(2,1)}), bf16[32,8,1024]{2,1,0:T(8,128)(2,1)S(1)}, u32[]{:S(2)}, u32[]{:S(2)}) async-start(bf16[32,8,1024]{2,1,0:T(8,128)(2,1)} %broadcast_in_dim.9), calls=%async_computation.1 | async-start | bytes 1048576 | tf_op jit(solution)/shard_map/all_to_all | solution.py:219
  51.2 12.4 %collective-permute-start.11 = (bf16[64,2048]{1,0:T(8,128)(2,1)S(1)}, bf16[64,2048]{1,0:T(8,128)(2,1)S(1)}, u32[]{:S(2)}, u32[]{:S(2)}) collective-permute-start(bf16[64,2048]{1,0:T(8,128)(2,1)S(1)} %select_select_fusion.1), channel_id=1, source_target_pairs={{0,16},{32,48},{64,80},{96,112},{128,144},{160,176},{192,208},{224... | collective-permute-start | bytes 786440 | tf_op jit(solution)/shard_map/ppermute | solution.py:42
  55.8 9.5 %collective-permute-start.10 = (bf16[64,2048]{1,0:T(8,128)(2,1)S(1)}, bf16[64,2048]{1,0:T(8,128)(2,1)}, u32[]{:S(2)}, u32[]{:S(2)}) collective-permute-start(bf16[64,2048]{1,0:T(8,128)(2,1)S(1)} %select_select_fusion.1), channel_id=1, source_target_pairs={{0,24},{32,56},{64,88},{96,120},{128,152},{160,184},{192,216},{224... | collective-permute-start | bytes 786440 | tf_op jit(solution)/shard_map/ppermute | solution.py:42
  57.9 12.1 %collective-permute-start.9 = (bf16[64,2048]{1,0:T(8,128)(2,1)S(1)}, bf16[64,2048]{1,0:T(8,128)(2,1)}, u32[]{:S(2)}, u32[]{:S(2)}) collective-permute-start(bf16[64,2048]{1,0:T(8,128)(2,1)S(1)} %select_select_fusion.1), channel_id=1, source_target_pairs={{0,8},{32,40},{64,72},{96,104},{128,136},{160,168},{192,200},{224,... | collective-permute-start | bytes 786440 | tf_op jit(solution)/shard_map/ppermute | solution.py:42
  70.0 18.0 %collective-permute-start.14 = (bf16[64,2048]{1,0:T(8,128)(2,1)S(1)}, bf16[64,2048]{1,0:T(8,128)(2,1)S(1)}, u32[]{:S(2)}, u32[]{:S(2)}) collective-permute-start(bf16[64,2048]{1,0:T(8,128)(2,1)S(1)} %select_select_fusion.after), channel_id=1, source_target_pairs={{0,6},{1,7},{2,0},{3,1},{4,2},{5,3},{6,4},{7,5},{8,14},{9,15},{10,... | collective-permute-start | bytes 786440 | tf_op jit(solution)/shard_map/ppermute | solution.py:19
  70.3 17.8 %collective-permute-start.13 = (bf16[64,2048]{1,0:T(8,128)(2,1)S(1)}, bf16[64,2048]{1,0:T(8,128)(2,1)S(1)}, u32[]{:S(2)}, u32[]{:S(2)}) collective-permute-start(bf16[64,2048]{1,0:T(8,128)(2,1)S(1)} %select_select_fusion.after), channel_id=1, source_target_pairs={{0,4},{1,5},{2,6},{3,7},{4,0},{5,1},{6,2},{7,3},{8,12},{9,13},{10,... | collective-permute-start | bytes 786440 | tf_op jit(solution)/shard_map/ppermute | solution.py:19
  70.7 18.7 %collective-permute-start.12 = (bf16[64,2048]{1,0:T(8,128)(2,1)S(1)}, bf16[64,2048]{1,0:T(8,128)(2,1)}, u32[]{:S(2)}, u32[]{:S(2)}) collective-permute-start(bf16[64,2048]{1,0:T(8,128)(2,1)S(1)} %select_select_fusion.after), channel_id=1, source_target_pairs={{0,2},{1,3},{2,4},{3,5},{4,6},{5,7},{6,0},{7,1},{8,10},{9,11},{10,... | collective-permute-start | bytes 786440 | tf_op jit(solution)/shard_map/ppermute | solution.py:19
  72.3 5.2 %copy-start.1 = (s32[11]{0:T(128)}, s32[11]{0:T(128)S(1)}, u32[]{:S(2)}) copy-start(s32[11]{0:T(128)S(1)} %stack.43.scal) | copy-start | bytes 136
  78.4 25.5 %all-to-all-start.2 = ((f16[32,8,1152]{2,1,0:T(8,128)(2,1)}), f16[32,8,1152]{2,1,0:T(8,128)(2,1)}, u32[]{:S(2)}, u32[]{:S(2)}) async-start(f16[32,8,1152]{2,1,0:T(8,128)(2,1)} %convert_element_type.6), calls=%async_computation.2 | async-start | bytes 1179648 | tf_op jit(solution)/shard_map/all_to_all | solution.py:229
  90.6 5.1 %copy-start.2 = (bf16[256,2048]{1,0:T(8,128)(2,1)}, bf16[256,2048]{1,0:T(8,128)(2,1)S(1)}, u32[]{:S(2)}) copy-start(bf16[256,2048]{1,0:T(8,128)(2,1)S(1)} %pad_maximum_fusion.1.refs_2_.refs_6_) | copy-start | bytes 3145732
  90.6 5.1 %collective-permute-start.15 = (bf16[256,2048]{1,0:T(8,128)(2,1)S(1)}, bf16[256,2048]{1,0:T(8,128)(2,1)}, u32[]{:S(2)}, u32[]{:S(2)}) collective-permute-start(bf16[256,2048]{1,0:T(8,128)(2,1)S(1)} %pad_maximum_fusion.1.refs_2_.refs_6_), channel_id=1, source_target_pairs={{0,1},{1,0},{2,3},{3,2},{4,5},{5,4},{6,7},{7,6},{8,9},{9,8},{10,11... | collective-permute-start | bytes 3145736 | tf_op jit(solution)/shard_map/ppermute | solution.py:23
  106.4 26.5 %all-to-all-start.3 = ((bf16[32,8,1024]{2,1,0:T(8,128)(2,1)}), bf16[32,8,1024]{2,1,0:T(8,128)(2,1)S(1)}, u32[]{:S(2)}, u32[]{:S(2)}) async-start(bf16[32,8,1024]{2,1,0:T(8,128)(2,1)} %merge_parts.1), calls=%async_computation.3 | async-start | bytes 1048576 | tf_op jit(solution)/shard_map/all_to_all | solution.py:234
  (2 other events, 1.4 us)
